TPU v7x, 128 devices: a whole 4x4x4 slice. The times are simulated.
128 devices in a mesh: seq: 8 (over y, core), head: 16 (over x, z).
Axes of the slice: x: 4, y: 4, z: 4, core: 2. Of those that a mesh axis runs over, the one named last changes fastest.
Arguments:
- hidden_states: bfloat16 [64, 64, 8192], P('seq', None, 'head'), may hold values from -33 to 33
- span_group: int32 [64, 1], replicated, may hold values from 0 to 7; in each aligned block of 8 rows (0 to 7, 8 to 15, ...) at most 2 rows name the same one
- span_slot: int32 [64], replicated, may hold values from 0 to 7
- span_block: int32 [64], replicated, may hold values from 0 to 127
- prompt_len: int32 [64], P('seq'), may hold values from 4096 to 8192
- new_tokens: bfloat16 [2, 64, 8192], P(None, 'seq', 'head'), may hold values from -12 to 12
- norm_gain: bfloat16 [2, 8192], replicated, may hold values from 0.25 to 1.75
- w_q: bfloat16 [8192, 4096], P(None, 'head'), may hold values from -8 to 8
- w_kv: bfloat16 [8192, 2, 4096], P(None, None, 'head'), may hold values from -0.0625 to 0.0625
- w_o: bfloat16 [4096, 8192], P('head'), may hold values from -0.09375 to 0.09375
- w_gate_up: bfloat16 [8192, 2, 16384], P(None, None, ('seq', 'head')), may hold values from -0.0625 to 0.0625
- w_down: bfloat16 [16384, 8192], P(('seq', 'head')), may hold values from -0.1875 to 0.1875
Outputs:
- mixed: bfloat16 [2, 64, 8192], P(None, 'seq', 'head')
Inputs may be any that keep to these rules, and one draw needn't show every extreme that they name: `span_group`: among the 8 spans of one index of seq (rows of one device, in order), at most 2 name the same group.
All inputs are finite; a program needn't handle non-finite values.
Results may differ from a plain program's by a relative error of at most 0.015.
Values may be sent and summed in bfloat16 or wider, within the bound.
A program may use at most 128 MiB of HBM per device.

v0:
```python
import math

import jax
import jax.numpy as jnp
from jax import lax
from jax.sharding import PartitionSpec as P

D = 8192
HD = 128
C = 64
CD = 8
CAP = 2


EPS = 1e-05
THETA = 10000.0
MASKED = -1e30


def rope_angles(positions):
    half_dim = HD // 2
    freqs = jnp.exp(jnp.arange(half_dim).astype(jnp.float32) * (-2.0 * math.log(THETA) / HD))
    angles = positions.astype(jnp.float32)[..., None] * freqs
    return (jnp.cos(angles), jnp.sin(angles))


def rotate(vectors, cosine, sine_table):
    half_dim = HD // 2
    first_half = vectors[..., :half_dim]
    second_half = vectors[..., half_dim:]
    cosine = cosine[..., None, :]
    sine_table = sine_table[..., None, :]
    return jnp.concatenate(
        [
            first_half * cosine - second_half * sine_table,
            first_half * sine_table + second_half * cosine,
        ],
        axis=-1,
    )


def normalize(values, mean_square, gain_part):
    return (values * lax.rsqrt(mean_square + EPS)[..., None] * gain_part).astype(jnp.bfloat16)


def pack_slots(selected_slots, incoming_blocks):
    return jnp.einsum(
        "nju,uak->njak", selected_slots, incoming_blocks, preferred_element_type=jnp.float32
    ).astype(jnp.bfloat16)


def attend(query_rows, cached_key_rows, cached_value_rows, new_keys, new_values, allowed):
    attention_score_scale = 1.0 / math.sqrt(HD)
    step_count = query_rows.shape[0]
    cached_entries = (
        jnp.einsum(
            "unij,oij->iuno", query_rows, cached_key_rows, preferred_element_type=jnp.float32
        )
        * attention_score_scale
    )
    cached_entries = jnp.where(allowed[None, None], cached_entries, MASKED)
    fresh = (
        jnp.einsum("srhd,urhd->hsru", query_rows, new_keys, preferred_element_type=jnp.float32)
        * attention_score_scale
    )
    causal = jnp.arange(step_count)[None, :] <= jnp.arange(step_count)[:, None]
    fresh = jnp.where(causal[None, :, None, :], fresh, MASKED)
    top_score = jnp.maximum(jnp.max(cached_entries, axis=-1), jnp.max(fresh, axis=-1))[..., None]
    cached_exp = jnp.exp(cached_entries - top_score)
    fresh_exp = jnp.exp(fresh - top_score)
    totals = jnp.sum(cached_exp, axis=-1, keepdims=True) + jnp.sum(
        fresh_exp, axis=-1, keepdims=True
    )
    cached_probability = (cached_exp / totals).astype(jnp.bfloat16)
    fresh_prob = (fresh_exp / totals).astype(jnp.bfloat16)
    summed_output = jnp.einsum(
        "gfxv,vgw->fxgw", cached_probability, cached_value_rows, preferred_element_type=jnp.float32
    )
    summed_output = summed_output + jnp.einsum(
        "hsru,urhd->srhd", fresh_prob, new_values, preferred_element_type=jnp.float32
    )
    return summed_output.astype(jnp.bfloat16)


def local(
    hidden_states,
    span_group,
    span_slot,
    span_block,
    prompt_len,
    new_tokens,
    norm_gain,
    w_q,
    w_kv,
    w_o,
    w_gate_up,
    w_down,
):
    seq_count = lax.axis_size("seq")
    head_count = lax.axis_size("head")
    my_group = lax.axis_index("seq")
    my_head = lax.axis_index("head")
    part_width = D // head_count
    inner_dev = w_q.shape[1]
    heads_dev = inner_dev // HD
    step_count = new_tokens.shape[0]
    req_dev = new_tokens.shape[1]
    gain_full = norm_gain.astype(jnp.float32)
    gain_attn = lax.dynamic_slice_in_dim(gain_full[0], my_head * part_width, part_width, 0)
    kv_flat = w_kv.reshape(D, 2 * inner_dev)
    all_groups = span_group[:, 0].reshape(seq_count, CD)
    all_slots = span_slot.reshape(seq_count, CD)
    all_blocks = span_block.reshape(seq_count, CD)
    span_order = jnp.arange(CD)
    earlier = span_order[None, :] < span_order[:, None]
    same_dest = all_groups[:, :, None] == all_groups[:, None, :]
    send_ranks = jnp.sum((same_dest & earlier[None]).astype(jnp.int32), axis=2)
    dest_iota = jnp.arange(seq_count)
    slot_iota = jnp.arange(CAP)
    own_groups = lax.dynamic_index_in_dim(all_groups, my_group, 0, keepdims=False)
    own_ranks = lax.dynamic_index_in_dim(send_ranks, my_group, 0, keepdims=False)
    sending = (own_groups[None, None, :] == dest_iota[:, None, None]) & (
        own_ranks[None, None, :] == slot_iota[None, :, None]
    )
    send_pick = sending.astype(jnp.bfloat16)
    arriving = (all_groups[:, None, :] == my_group) & (
        send_ranks[:, None, :] == slot_iota[None, :, None]
    )
    occupied = jnp.any(arriving, axis=2)
    arrived_slot = jnp.sum(jnp.where(arriving, all_slots[:, None, :], 0), axis=2)
    arrived_block = jnp.sum(jnp.where(arriving, all_blocks[:, None, :], 0), axis=2)
    offsets = jnp.arange(C)
    arrived_positions = (arrived_block[:, :, None] * C + offsets).reshape(-1)
    arrived_owner = jnp.broadcast_to(arrived_slot[:, :, None], (seq_count, CAP, C)).reshape(-1)
    arrived_live = jnp.broadcast_to(occupied[:, :, None], (seq_count, CAP, C)).reshape(-1)
    packed = pack_slots(send_pick, hidden_states)
    arrived = lax.all_to_all(packed, "seq", split_axis=0, concat_axis=0, tiled=True)
    arrived_float = arrived.reshape(-1, part_width).astype(jnp.float32)
    squares = lax.psum(jnp.sum(arrived_float * arrived_float, axis=1), "head")
    normed_rows = normalize(arrived_float, squares / D, gain_attn)
    kv_sum = jnp.dot(
        lax.all_gather(normed_rows, "head", axis=1, tiled=True),
        kv_flat,
        preferred_element_type=jnp.float32,
    )
    cache_cos, cache_sin = rope_angles(arrived_positions)
    cached_key_rows = rotate(
        kv_sum[:, :inner_dev].reshape(-1, heads_dev, HD), cache_cos, cache_sin
    ).astype(jnp.bfloat16)
    cached_value_rows = kv_sum[:, inner_dev:].reshape(-1, heads_dev, HD).astype(jnp.bfloat16)
    token_full = lax.all_gather(new_tokens, "head", axis=2, tiled=True)
    token_float = token_full.astype(jnp.float32)
    normed_tokens = normalize(
        token_float, jnp.mean(token_float * token_float, axis=-1), gain_full[0]
    )
    flat_tokens = normed_tokens.reshape(-1, D)
    token_positions = prompt_len[None, :] + jnp.arange(step_count, dtype=jnp.int32)[:, None]
    token_cos, token_sin = rope_angles(token_positions)
    query_rows = rotate(
        jnp.dot(flat_tokens, w_q, preferred_element_type=jnp.float32).reshape(
            step_count, req_dev, heads_dev, HD
        ),
        token_cos,
        token_sin,
    ).astype(jnp.bfloat16)
    fresh_kv = jnp.dot(flat_tokens, kv_flat, preferred_element_type=jnp.float32).reshape(
        step_count, req_dev, 2, heads_dev, HD
    )
    new_keys = rotate(fresh_kv[:, :, 0], token_cos, token_sin).astype(jnp.bfloat16)
    new_values = fresh_kv[:, :, 1].astype(jnp.bfloat16)
    allowed = (
        (arrived_owner[None, :] == jnp.arange(req_dev)[:, None])
        & (arrived_positions[None, :] < prompt_len[:, None])
        & arrived_live[None, :]
    )
    attended = attend(query_rows, cached_key_rows, cached_value_rows, new_keys, new_values, allowed)
    attn_part = jnp.dot(
        attended.reshape(-1, inner_dev), w_o, preferred_element_type=jnp.float32
    ).reshape(step_count, req_dev, D)
    attn_full = lax.psum(attn_part, "head")
    resid_full = token_float + attn_full
    normed_ffn = normalize(resid_full, jnp.mean(resid_full * resid_full, axis=-1), gain_full[1])
    resid_own = lax.dynamic_slice_in_dim(resid_full, my_head * part_width, part_width, 2)
    ffn_input = lax.all_gather(normed_ffn, "seq", axis=1, tiled=True)
    grouped = ffn_input.reshape(step_count, seq_count, req_dev, D)
    gate_up = jnp.einsum("tgrd,dkf->tgrkf", grouped, w_gate_up, preferred_element_type=jnp.float32)
    activated = (jax.nn.silu(gate_up[:, :, :, 0]) * gate_up[:, :, :, 1]).astype(jnp.bfloat16)
    down_parts = w_down.reshape(w_down.shape[0], head_count, part_width)
    terms = jnp.einsum(
        "tgrf,fjd->gjtrd", activated, down_parts, preferred_element_type=jnp.float32
    ).reshape(-1, part_width)
    ffn_own = lax.psum_scatter(terms, ("seq", "head"), scatter_dimension=0, tiled=True).reshape(
        step_count, req_dev, part_width
    )
    return (resid_own + ffn_own).astype(jnp.bfloat16)


def solution(mesh):
    placed = (
        P("seq", None, "head"),
        P(),
        P(),
        P(),
        P("seq"),
        P(None, "seq", "head"),
        P(),
        P(None, "head"),
        P(None, None, "head"),
        P("head", None),
        P(None, None, ("seq", "head")),
        P(("seq", "head"), None),
    )
    return jax.shard_map(
        local, mesh=mesh, in_specs=placed, out_specs=P(None, "seq", "head"), check_vma=False
    )
```

profile of v0, /device:TPU:0, one launch (start us, length us, event | category | flops | bytes accessed | tf_op | source)
XLA Modules:
  0.0 990.8 jit_solution(2282405064455839671)
XLA Ops:
  6.5 0.5 broadcast.215
  7.1 1.3 reduce.4
  8.5 0.3 convert_reduce_fusion
  8.8 1.5 convolution_convert_fusion
  10.3 1.3 copy.118
  11.6 4.6 all-to-all-start
  16.3 15.8 %all-to-all-done = bf16[8,2,64,512]{3,2,1,0:T(8,128)(2,1)S(1)} async-done(((bf16[8,2,64,512]{3,2,1,0:T(8,128)(2,1)}), bf16[8,2,64,512]{3,2,1,0:T(8,128)(2,1)S(1)}, u32[]{:S(2)}, u32[]{:S(2)}) %all-to-all-start) | async-done | bytes 1048608 | tf_op jit(solution)/shard_map/all_to_all | solution.py:137
  32.1 0.3 multiply_reduce_fusion
  32.5 41.7 %psum.14 = f32[1024]{0:T(1024)S(1)} all-reduce(f32[1024]{0:T(1024)S(1)} %reduce_sum.76), channel_id=1, replica_groups=mesh['seq'=8,'head'=16] {'head'}, use_global_device_ids=true, to_apply=%region_2.3 | all-reduce | flops 1024 | bytes 8192 | tf_op jit(solution)/shard_map/psum | solution.py:139
  74.2 1.3 fusion.7
  75.5 8.0 copy.166
  83.5 11.4 %copy.128 = bf16[512,8192]{1,0:T(8,128)(2,1)} copy(bf16[512,8192]{0,1:T(8,128)(2,1)} %bitcast.110) | data formatting | bytes 16777216 | tf_op jit(solution)/shard_map/dot_general | solution.py:166
  95.0 6.4 copy.156
  101.3 21.2 %all_gather.9 = bf16[2,8,8192]{2,1,0:T(8,128)(2,1)S(1)} all-gather(bf16[2,8,512]{2,1,0:T(8,128)(2,1)S(1)} %copy-done.3), channel_id=1, replica_groups=mesh['seq'=8,'head'=16] {'head'}, dimensions={2}, use_global_device_ids=true | all-gather | bytes 278528 | tf_op jit(solution)/shard_map/all_gather | solution.py:151
  122.6 0.2 fusion.13
  122.8 0.1 multiply_cosine_fusion.1
  122.9 6.1 fusion.20
  129.1 1.2 fusion.22
  130.3 0.1 subtract_convert_fusion.1
  130.5 0.2 fusion.58
  130.9 0.2 select_reduce_fusion.1
  131.5 0.2 fusion.41
  131.7 0.1 copy.123
  131.9 0.1 and.60
  132.1 2.9 multiply_cosine_fusion
  135.0 57.3 %all-gather.3.cloned.1.call-done = bf16[1024,8192]{1,0:T(8,128)(2,1)} async-done(((bf16[1024,512]{1,0:T(8,128)(2,1)}), bf16[1024,8192]{1,0:T(8,128)(2,1)}) %all-gather.3.cloned.1.call-update) | async-done | bytes 16777232 | tf_op jit(solution)/shard_map/all_gather | solution.py:142
  192.3 17.2 %fusion.59 = f32[1024,512]{0,1:T(8,128)S(1)} fusion(bf16[1024,8192]{1,0:T(8,128)(2,1)} %all-gather.3.cloned.1.call-done, bf16[8192,512]{1,0:T(8,128)(2,1)} %bitcast.111), kind=kOutput, calls=%fused_computation.110 | convolution fusion | flops 8589934592 | bytes 27262976 | tf_op jit(solution)/shard_map/dot_general | solution.py:141
  209.6 0.9 slice.96
  210.5 0.3 copy.163
  210.9 0.3 copy.164
  211.2 1.4 subtract_convert_fusion
  212.6 0.5 fusion.57
  213.1 0.1 copy.133
  213.3 0.2 fusion.26
  213.6 0.2 fusion.44
  213.8 0.3 fusion.12
  214.1 3.7 fusion.2
  217.9 84.3 %all-reduce.2.cloned.1.call-done = f32[2,8,8192]{2,1,0:T(8,128)} async-done(((f32[2,8,8192]{2,1,0:T(8,128)}), f32[2,8,8192]{2,1,0:T(8,128)}) %all-reduce.2.cloned.1.call-update) | async-done | bytes 524304 | tf_op jit(solution)/shard_map/psum | solution.py:180
  302.2 1.2 multiply_reduce_fusion.1
  303.4 0.8 multiply_convert_fusion
  304.3 0.3 reduce-scatter.2.cloned.1.call-start
  304.5 2.4 copy.167
  307.0 21.9 %all-gather.5.cloned.1.call-done = bf16[2,64,8192]{2,1,0:T(8,128)(2,1)} async-done(((bf16[2,8,8192]{2,1,0:T(8,128)(2,1)}), bf16[2,64,8192]{2,1,0:T(8,128)(2,1)}) %all-gather.5.cloned.1.call-update) | async-done | bytes 2097168 | tf_op jit(solution)/shard_map/all_gather | solution.py:184
  328.9 3.5 fusion
  332.4 2.7 convolution_bitcast_fusion
  335.1 2.6 copy.143
  337.7 645.2 %reduce-scatter.2.cloned.1.call-done = f32[16,512]{1,0:T(8,128)} async-done(((f32[2048,512]{1,0:T(8,128)}), f32[16,512]{1,0:T(8,128)}) %reduce-scatter.2.cloned.1.call-update) | async-done | bytes 32784 | tf_op jit(solution)/shard_map/reduce_scatter | solution.py:192
  982.9 1.4 fusion.31
  (59 shorter events, 1.9 us)
Async XLA Ops:
  6.5 9.7 copy-start.2
  11.6 20.5 %all-to-all-start = ((bf16[8,2,64,512]{3,2,1,0:T(8,128)(2,1)}), bf16[8,2,64,512]{3,2,1,0:T(8,128)(2,1)S(1)}, u32[]{:S(2)}, u32[]{:S(2)}) async-start(bf16[8,2,64,512]{3,2,1,0:T(8,128)(2,1)} %copy.118), calls=%async_computation | async-start | bytes 2097152 | tf_op jit(solution)/shard_map/all_to_all | solution.py:137
  16.2 176.1 %all-gather.3.cloned.1.call-start = ((), (), s32[]{:S(2)}) async-start(), calls=%async_computation.2 | async-start | bytes 17825792 | tf_op jit(solution)/shard_map/all_gather | solution.py:142
  75.5 226.7 %all-reduce.2.cloned.1.call-start = ((), (), s32[]{:S(2)}) async-start(), calls=%async_computation.3 | async-start | bytes 1048576 | tf_op jit(solution)/shard_map/psum | solution.py:180
  94.9 6.4 copy-start.3
  94.9 27.8 %copy-start.6 = (s32[8]{0:T(128)S(1)}, s32[8]{0:T(128)}, u32[]{:S(2)}) copy-start(s32[8]{0:T(128)} %param.16) | copy-start | bytes 100
  122.9 6.2 copy-start
  129.0 1.7 copy-start.4
  129.0 1.8 copy-start.5
  211.2 2.6 copy-start.1
  217.8 111.1 %all-gather.5.cloned.1.call-start = ((), (), s32[]{:S(2)}) async-start(), calls=%async_computation.4 | async-start | bytes 2359296 | tf_op jit(solution)/shard_map/all_gather | solution.py:184
  304.3 678.6 %reduce-scatter.2.cloned.1.call-start = ((), (), s32[]{:S(2)}) async-start(), calls=%async_computation.5 | async-start | bytes 4227072 | tf_op jit(solution)/shard_map/reduce_scatter | solution.py:192
Sparse Core Ops, SparseCore 0:
  75.6 116.6 all-gather.2
  217.9 84.2 all-reduce.1
  304.4 24.4 all-gather.4
  337.8 645.0 reduce-scatter.1
where the time goes:
time: 992 us; the launch traced here: 991 us
  waiting for transfers between devices  825 us (83%)
  blocking collectives  62.9 us (6%)
  matrix products  37.1 us (4%)
  local copies, waits for them, and re-layouts  35.7 us (4%)
  between operations  13.4 us (1%)
  other arithmetic  12.2 us (1%)
    reduce_scatter x1, waiting for transfers between devices, local(): lax.psum_scatter(terms, ('seq', 'head'), scatter_dimension=0, tiled=True)  645 us
    psum x1, waiting for transfers between devices, local(): attn_full = lax.psum(attn_part, 'head')  84.3 us
    all_gather x1, waiting for transfers between devices, local(): lax.all_gather(normed_rows, 'head', axis=1, tiled=True)  57.3 us
    psum x1, blocking collectives, local(): squares = lax.psum(jnp.sum(arrived_float * arrived_float, axis=1), 'head')  41.7 us
    all_gather x1, waiting for transfers between devices, local(): ffn_input = lax.all_gather(normed_ffn, 'seq', axis=1, tiled=True)  21.9 us
    all_gather x1, blocking collectives, local(): token_full = lax.all_gather(new_tokens, 'head', axis=2, tiled=True)  21.2 us
  transfers between devices with their start and end apart: 5, of which 5 were waited for; matrix products, arithmetic and copies ran while one was open for 4% of the time, Pallas kernels for 0%

commit v1 on v0

--- a/solution.py
+++ b/solution.py
@@ -3,6 +3,8 @@
 import jax
 import jax.numpy as jnp
 from jax import lax
+from jax.experimental import pallas as pl
+from jax.experimental.pallas import tpu as pltpu
 from jax.sharding import PartitionSpec as P
 
 D = 8192
@@ -15,6 +17,254 @@
 EPS = 1e-05
 THETA = 10000.0
 MASKED = -1e30
+
+
+MESH = pl.DeviceIdType.MESH
+BF = jnp.bfloat16
+F32 = jnp.float32
+
+
+def tail_kernel(
+    att_ref, tok_ref, gain_ref, wo_hbm, wgu_hbm, wd_hbm, out_ref,
+    wo, wgu, wd, send_a, recv_a, rows, own_terms, send_d1, recv_d1, send_d2, recv_d2, send_d3, recv_d3, res,
+    wsem, sa, ra, s1, r1, s2, r2, s3, r3, sd1, rd1, sd2, rd2, sd3, rd3,
+):
+    s = lax.axis_index("seq")
+    h = lax.axis_index("head")
+    y = s // 2
+    c = lax.rem(s, 2)
+    slot = c * 4 + y
+    pair = s + 1 - 2 * c
+
+    def at_head(k):
+        return lax.rem(h + k, 16)
+
+    barrier = pltpu.get_barrier_semaphore()
+
+    @pl.loop(1, 16)
+    def _(k):
+        pl.semaphore_signal(barrier, inc=1, device_id=(s, at_head(k)), device_id_type=MESH)
+
+    @pl.loop(1, 8)
+    def _(k):
+        pl.semaphore_signal(barrier, inc=1, device_id=(lax.rem(s + k, 8), h), device_id_type=MESH)
+
+    def weight_copies(j):
+        cols = pl.ds(pl.multiple_of(j * 512, 512), 512)
+        return (
+            pltpu.make_async_copy(wo_hbm.at[:, cols], wo.at[j], wsem.at[0, j]),
+            pltpu.make_async_copy(wgu_hbm.at[cols], wgu.at[j], wsem.at[1, j]),
+            pltpu.make_async_copy(wd_hbm.at[:, cols], wd.at[j], wsem.at[2, j]),
+        )
+
+    for which in range(3):
+        @pl.loop(0, 16)
+        def _(j):
+            weight_copies(j)[which].start()
+
+    pl.semaphore_wait(barrier, 22)
+
+    def remote(src, dst, ssem, rsem, device):
+        return pltpu.make_async_remote_copy(
+            src_ref=src, dst_ref=dst, send_sem=ssem, recv_sem=rsem, device_id=device, device_id_type=MESH
+        )
+
+    @pl.loop(0, 16)
+    def _(j):
+        weight_copies(j)[0].wait()
+
+    def copy_a(k):
+        t = at_head(k)
+        return remote(send_a.at[t], recv_a.at[h], sa.at[t], ra.at[h], (s, t))
+
+    def came_a(k):
+        f = at_head(16 - k)
+        return remote(send_a.at[f], recv_a.at[f], sa.at[f], ra.at[f], (s, f))
+
+    @pl.loop(1, 16)
+    def _(k):
+        t = at_head(k)
+        send_a[t] = jnp.dot(att_ref[...], wo[t], preferred_element_type=F32).astype(BF)
+        copy_a(k).start()
+
+    res[...] = tok_ref[...].astype(F32) + jnp.dot(att_ref[...], wo[h], preferred_element_type=F32)
+
+    @pl.loop(1, 16)
+    def _(k):
+        came_a(k).wait_recv()
+        res[...] += recv_a[at_head(16 - k)].astype(F32)
+
+    rows[h, slot] = res[...].astype(BF)
+
+    def copy_1(k):
+        t = lax.rem(s + k, 8)
+        return remote(rows.at[h, slot], rows.at[h, slot], s1.at[t], r1.at[s], (t, h))
+
+    def came_1(k):
+        f = lax.rem(s + 8 - k, 8)
+        place = lax.rem(f, 2) * 4 + f // 2
+        return remote(rows.at[h, place], rows.at[h, place], s1.at[f], r1.at[f], (f, h))
+
+    @pl.loop(1, 8)
+    def _(k):
+        copy_1(k).start()
+
+    @pl.loop(1, 8)
+    def _(k):
+        came_1(k).wait_recv()
+
+    mine = pl.ds(c * 4, 4)
+    other = pl.ds(4 - c * 4, 4)
+
+    def copy_2(k):
+        t = at_head(k)
+        return remote(rows.at[h, mine], rows.at[h, mine], s2.at[t], r2.at[h], (s, t))
+
+    def came_2(k):
+        f = at_head(16 - k)
+        return remote(rows.at[f, mine], rows.at[f, mine], s2.at[f], r2.at[f], (s, f))
+
+    def copy_3(k):
+        f = at_head(16 - k)
+        return remote(rows.at[f, mine], rows.at[f, mine], s3.at[f], r3.at[f], (pair, h))
+
+    def came_3(k):
+        f = at_head(16 - k)
+        return remote(rows.at[f, other], rows.at[f, other], s3.at[f], r3.at[f], (pair, h))
+
+    @pl.loop(1, 16)
+    def _(k):
+        copy_2(k).start()
+
+    @pl.loop(0, 16)
+    def _(j):
+        weight_copies(j)[1].wait()
+        weight_copies(j)[2].wait()
+
+    def block(j, carry):
+        acc, squares = carry
+        part = rows[j].reshape(128, 512).astype(F32)
+        sq = part * part
+        squares = squares + (sq[:, 0:128] + sq[:, 128:256]) + (sq[:, 256:384] + sq[:, 384:512])
+        scaled = (part * gain_ref[j]).astype(BF)
+        return acc + jnp.dot(scaled, wgu[j], preferred_element_type=F32), squares
+
+    carry = block(h, (jnp.zeros((128, 256), F32), jnp.zeros((128, 128), F32)))
+
+    def step(k, carry):
+        came_2(k).wait_recv()
+        copy_3(k).start()
+        came_3(k).wait_recv()
+        return block(at_head(16 - k), carry)
+
+    acc, squares = lax.fori_loop(1, 16, step, carry)
+    scale = lax.rsqrt(jnp.sum(squares, axis=1, keepdims=True) / D + EPS)
+    gate = acc[:, 0:128] * scale
+    up = acc[:, 128:256] * scale
+    act = (gate / (1.0 + jnp.exp(-gate)) * up).astype(BF)
+
+    def copy_d1(t):
+        return remote(send_d1.at[t], recv_d1.at[t], sd1.at[t], rd1.at[t], (pair, h))
+
+    def copy_d2(t):
+        return remote(send_d2.at[t], recv_d2.at[h], sd2.at[t], rd2.at[h], (s, t))
+
+    def came_d2(f):
+        return remote(send_d2.at[f], recv_d2.at[f], sd2.at[f], rd2.at[f], (s, f))
+
+    @pl.loop(0, 16)
+    def _(k):
+        t = at_head(k + 1)
+        terms = jnp.dot(act, wd[t], preferred_element_type=F32)
+        low, high = terms[0:64], terms[64:128]
+        own_terms[t] = jnp.where(c == 0, low, high)
+        send_d1[t] = jnp.where(c == 0, high, low).astype(BF)
+        copy_d1(t).start()
+
+    @pl.loop(0, 15)
+    def _(k):
+        t = at_head(k + 1)
+        copy_d1(t).wait_recv()
+        send_d2[t] = (own_terms[t] + recv_d1[t].astype(F32)).astype(BF)
+        copy_d2(t).start()
+
+    copy_d1(h).wait_recv()
+    own_terms[h] = own_terms[h] + recv_d1[h].astype(F32)
+
+    @pl.loop(1, 16)
+    def _(k):
+        f = at_head(16 - k)
+        came_d2(f).wait_recv()
+        own_terms[h] += recv_d2[f].astype(F32)
+
+    def copy_d3(k):
+        t = lax.rem(y + k, 4)
+        return remote(send_d3.at[t], recv_d3.at[y], sd3.at[t], rd3.at[y], (t * 2 + c, h))
+
+    def came_d3(k):
+        f = lax.rem(y + 4 - k, 4)
+        return remote(send_d3.at[f], recv_d3.at[f], sd3.at[f], rd3.at[f], (f * 2 + c, h))
+
+    send_d3[...] = own_terms[h].reshape(4, 16, 512).astype(BF)
+    for k in range(1, 4):
+        copy_d3(k).start()
+    total = res[...] + own_terms[h, pl.ds(pl.multiple_of(y * 16, 16), 16)]
+    for k in range(1, 4):
+        came_d3(k).wait_recv()
+        total = total + recv_d3[lax.rem(y + 4 - k, 4)].astype(F32)
+    out_ref[...] = total.astype(BF)
+
+    @pl.loop(1, 16)
+    def _(k):
+        copy_a(k).wait_send()
+        copy_2(k).wait_send()
+        copy_3(k).wait_send()
+        copy_d1(at_head(k)).wait_send()
+        copy_d2(at_head(k)).wait_send()
+
+    copy_d1(h).wait_send()
+
+    @pl.loop(1, 8)
+    def _(k):
+        copy_1(k).wait_send()
+
+    for k in range(1, 4):
+        copy_d3(k).wait_send()
+
+
+def tail(attended, tokens, gain, w_o, w_gu, w_d):
+    vmem = pl.BlockSpec(memory_space=pltpu.VMEM)
+    hbm = pl.BlockSpec(memory_space=pl.ANY)
+    dma = pltpu.SemaphoreType.DMA
+    return pl.pallas_call(
+        tail_kernel,
+        name="tail",
+        out_shape=jax.ShapeDtypeStruct((16, 512), BF),
+        in_specs=[vmem, vmem, vmem, hbm, hbm, hbm],
+        out_specs=vmem,
+        scratch_shapes=[
+            pltpu.VMEM((16, 256, 512), BF),
+            pltpu.VMEM((16, 512, 256), BF),
+            pltpu.VMEM((16, 128, 512), BF),
+            pltpu.VMEM((16, 16, 512), BF),
+            pltpu.VMEM((16, 16, 512), BF),
+            pltpu.VMEM((16, 8, 16, 512), BF),
+            pltpu.VMEM((16, 64, 512), F32),
+            pltpu.VMEM((16, 64, 512), BF),
+            pltpu.VMEM((16, 64, 512), BF),
+            pltpu.VMEM((16, 64, 512), BF),
+            pltpu.VMEM((16, 64, 512), BF),
+            pltpu.VMEM((4, 16, 512), BF),
+            pltpu.VMEM((4, 16, 512), BF),
+            pltpu.VMEM((16, 512), F32),
+            dma((3, 16)),
+            dma((16,)), dma((16,)), dma((8,)), dma((8,)), dma((16,)), dma((16,)), dma((16,)), dma((16,)),
+            dma((16,)), dma((16,)), dma((16,)), dma((16,)), dma((4,)), dma((4,)),
+        ],
+        compiler_params=pltpu.CompilerParams(
+            collective_id=1, has_side_effects=True, vmem_limit_bytes=56 * 2**20
+        ),
+    )(attended, tokens, gain, w_o, w_gu, w_d)
 
 
 def rope_angles(positions):
@@ -174,25 +424,15 @@
         & arrived_live[None, :]
     )
     attended = attend(query_rows, cached_key_rows, cached_value_rows, new_keys, new_values, allowed)
-    attn_part = jnp.dot(
-        attended.reshape(-1, inner_dev), w_o, preferred_element_type=jnp.float32
-    ).reshape(step_count, req_dev, D)
-    attn_full = lax.psum(attn_part, "head")
-    resid_full = token_float + attn_full
-    normed_ffn = normalize(resid_full, jnp.mean(resid_full * resid_full, axis=-1), gain_full[1])
-    resid_own = lax.dynamic_slice_in_dim(resid_full, my_head * part_width, part_width, 2)
-    ffn_input = lax.all_gather(normed_ffn, "seq", axis=1, tiled=True)
-    grouped = ffn_input.reshape(step_count, seq_count, req_dev, D)
-    gate_up = jnp.einsum("tgrd,dkf->tgrkf", grouped, w_gate_up, preferred_element_type=jnp.float32)
-    activated = (jax.nn.silu(gate_up[:, :, :, 0]) * gate_up[:, :, :, 1]).astype(jnp.bfloat16)
-    down_parts = w_down.reshape(w_down.shape[0], head_count, part_width)
-    terms = jnp.einsum(
-        "tgrf,fjd->gjtrd", activated, down_parts, preferred_element_type=jnp.float32
-    ).reshape(-1, part_width)
-    ffn_own = lax.psum_scatter(terms, ("seq", "head"), scatter_dimension=0, tiled=True).reshape(
-        step_count, req_dev, part_width
-    )
-    return (resid_own + ffn_own).astype(jnp.bfloat16)
+    out = tail(
+        attended.reshape(-1, inner_dev),
+        new_tokens.reshape(-1, part_width),
+        gain_full[1].reshape(head_count, 1, part_width),
+        w_o,
+        w_gate_up.reshape(D, -1),
+        w_down,
+    )
+    return out.reshape(step_count, req_dev, part_width)
 
 
 def solution(mesh):

time: 992 us -> 294 us (0.30)
  waiting for transfers between devices: 825 us -> 67.6 us
  Pallas kernels: 0 us -> 69.1 us
  matrix products: 37.1 us -> 27 us
    reduce_scatter x1 -> x0, waiting for transfers between devices: 645 us -> none  [local(): lax.psum_scatter(terms, ('seq', 'head'), scatter_dimension=0, tiled=True)]
    psum x1 -> x0, waiting for transfers between devices: 84.3 us -> none  [local(): attn_full = lax.psum(attn_part, 'head')]
    pallas_call x0 -> x1, Pallas kernels: none -> 69.1 us  [tail(): pl.pallas_call(tail_kernel, name='tail', out_shape=jax.ShapeDtypeStruct((...]
    all_gather x1 -> x0, waiting for transfers between devices: 21.9 us -> none  [local(): ffn_input = lax.all_gather(normed_ffn, 'seq', axis=1, tiled=True)]
    dot_general x3 -> x0, matrix products: 9.93 us -> none  [the longest x1 3.68 us: local(): jnp.dot(attended.reshape(-1, inner_dev), w_o, preferred_element_type=jnp....]
  transfers between devices with their start and end apart: 5 -> 2, of which waited for: 5 -> 2; matrix products, arithmetic and copies ran while one was open for 4% -> 15% of each run, Pallas kernels for 0% -> 0%
where the time goes in v1:
time: 294 us; the launch traced here: 292 us
  Pallas kernels  69.1 us (24%)
  waiting for transfers between devices  67.6 us (23%)
  blocking collectives  63 us (21%)
  local copies, waits for them, and re-layouts  38 us (13%)
  matrix products  27 us (9%)
  between operations  13.6 us (5%)
  other arithmetic  8.71 us (3%)
  starting transfers between devices  4.59 us (2%)
    pallas_call x1, Pallas kernels, tail(): pl.pallas_call(tail_kernel, name='tail', out_shape=jax.ShapeDtypeStruct((...  69.1 us
    all_gather x1, waiting for transfers between devices, local(): lax.all_gather(normed_rows, 'head', axis=1, tiled=True)  52.3 us
    psum x1, blocking collectives, local(): squares = lax.psum(jnp.sum(arrived_float * arrived_float, axis=1), 'head')  41.7 us
    all_gather x1, blocking collectives, local(): token_full = lax.all_gather(new_tokens, 'head', axis=2, tiled=True)  21.3 us
    dot_general x1, matrix products, local(): jnp.dot(lax.all_gather(normed_rows, 'head', axis=1, tiled=True), kv_flat,...  17.2 us
    unnamed x20, local copies, waits for them, and re-layouts  15.3 us
    all_to_all x1, waiting for transfers between devices, local(): lax.all_to_all(packed, 'seq', split_axis=0, concat_axis=0, tiled=True)  15.3 us
    dot_general x1, local copies, waits for them, and re-layouts, local(): jnp.dot(flat_tokens, kv_flat, preferred_element_type=jnp.float32)  11.4 us
  transfers between devices with their start and end apart: 2, of which 2 were waited for; matrix products, arithmetic and copies ran while one was open for 15% of the time, Pallas kernels for 0%

profile of v1, /device:TPU:0, one launch (start us, length us, event | category | flops | bytes accessed | tf_op | source)
XLA Modules:
  0.0 291.6 jit_solution(3671858391045784370)
XLA Ops:
  6.5 0.5 broadcast.200
  7.1 1.3 reduce.4
  8.5 0.3 convert_reduce_fusion
  8.8 1.5 convolution_convert_fusion
  10.3 1.3 copy.105
  11.6 4.6 %all-to-all-start = ((bf16[8,2,64,512]{3,2,1,0:T(8,128)(2,1)}), bf16[8,2,64,512]{3,2,1,0:T(8,128)(2,1)S(1)}, u32[]{:S(2)}, u32[]{:S(2)}) async-start(bf16[8,2,64,512]{3,2,1,0:T(8,128)(2,1)} %copy.105), calls=%async_computation | async-start | bytes 2097152 | tf_op jit(solution)/shard_map/all_to_all | solution.py:387
  16.2 0.6 fusion.43
  16.9 15.3 %all-to-all-done = bf16[8,2,64,512]{3,2,1,0:T(8,128)(2,1)S(1)} async-done(((bf16[8,2,64,512]{3,2,1,0:T(8,128)(2,1)}), bf16[8,2,64,512]{3,2,1,0:T(8,128)(2,1)S(1)}, u32[]{:S(2)}, u32[]{:S(2)}) %all-to-all-start) | async-done | bytes 1048608 | tf_op jit(solution)/shard_map/all_to_all | solution.py:387
  32.1 0.3 multiply_reduce_fusion
  32.4 0.1 reduce_sum.67
  32.5 41.7 %psum.7 = f32[1024]{0:T(1024)S(1)} all-reduce(f32[1024]{0:T(1024)S(1)} %reduce_sum.67), channel_id=1, replica_groups=mesh['seq'=8,'head'=16] {'head'}, use_global_device_ids=true, to_apply=%region_2.3 | all-reduce | flops 1024 | bytes 8192 | tf_op jit(solution)/shard_map/psum | solution.py:389
  74.2 1.3 fusion.1
  75.5 8.0 %copy.142 = bf16[1024,8,2,256]{3,1,2,0:T(8,128)(2,1)} copy(bf16[1024,8,2,256]{3,2,1,0:T(2,128)(2,1)} %bitcast.93) | data formatting | bytes 16777216
  83.7 0.2 select_reduce_fusion.1
  83.8 0.1 copy.109
  84.0 0.1 add.92
  84.1 11.4 %copy.115 = bf16[512,8192]{1,0:T(8,128)(2,1)} copy(bf16[512,8192]{0,1:T(8,128)(2,1)} %bitcast.88) | data formatting | bytes 16777216 | tf_op jit(solution)/shard_map/dot_general | solution.py:416
  95.5 6.4 %copy.136 = bf16[256,8192]{1,0:T(8,128)(2,1)} copy(bf16[256,8192]{0,1:T(8,128)(2,1)} %bitcast.94) | data formatting | bytes 8388608 | tf_op jit(solution)/shard_map/dot_general | solution.py:410
  102.1 0.1 fusion.29
  102.3 0.1 copy.110
  102.4 0.1 and.60
  102.5 21.3 %all_gather.7 = bf16[2,8,8192]{2,1,0:T(8,128)(2,1)S(1)} all-gather(bf16[2,8,512]{2,1,0:T(8,128)(2,1)S(1)} %copy-done.3), channel_id=1, replica_groups=mesh['seq'=8,'head'=16] {'head'}, dimensions={2}, use_global_device_ids=true | all-gather | bytes 278528 | tf_op jit(solution)/shard_map/all_gather | solution.py:401
  123.9 0.2 fusion.7
  124.0 0.1 multiply_cosine_fusion.1
  124.2 6.0 %fusion.14 = f32[2,8,2,2,128]{4,1,3,2,0:T(8,128)S(1)} fusion(bf16[2,2,128,8192,1]{3,2,1,0,4:T(8,128)(2,1)} %bitcast.90, bf16[2,8,8192]{2,1,0:T(8,128)(2,1)S(1)} %all_gather.7, f32[8192]{0:T(1024)S(1)} %bitcast.97, f32[2,8]{1,0:T(2,128)S(1)} %add_rsqrt_fusion.1), kind=kOutput, calls=%fused_computation.29 | convolution fusion | flops 134742016 | bytes 8716352 | tf_op jit(solution)/shard_map/dot_general | solution.py:416
  130.2 1.2 fusion.16
  131.4 0.1 subtract_convert_fusion.1
  131.5 0.1 pad_maximum_fusion
  131.5 0.2 fusion.45
  131.7 0.1 copy.119
  131.8 4.7 %copy.167 = bf16[1024,8,2,128]{3,1,2,0:T(8,128)(2,1)} copy(bf16[1024,8,2,128]{3,2,1,0:T(2,128)(2,1)} %bitcast.95) | data formatting | bytes 8388608
  136.6 3.0 %multiply_cosine_fusion = (f32[1024,64]{1,0:T(8,128)S(1)}, f32[1024,64]{1,0:T(8,128)}) fusion(f32[64]{0:T(128)S(1)} %multiply_exponential_fusion, f32[1024]{0:T(1024)S(1)} %convert_element_type.88), kind=kLoop, calls=%fused_computation.18 | loop fusion | flops 65536 | bytes 528640 | tf_op jit(solution)/shard_map/cos | solution.py:274
  139.5 52.3 %all-gather.2.cloned.1.call-done = bf16[1024,8192]{1,0:T(8,128)(2,1)} async-done(((bf16[1024,512]{1,0:T(8,128)(2,1)}), bf16[1024,8192]{1,0:T(8,128)(2,1)}) %all-gather.2.cloned.1.call-update) | async-done | bytes 16777232 | tf_op jit(solution)/shard_map/all_gather | solution.py:392
  191.9 17.2 %fusion.46 = f32[1024,512]{0,1:T(8,128)S(1)} fusion(bf16[1024,8192]{1,0:T(8,128)(2,1)} %all-gather.2.cloned.1.call-done, bf16[8192,512]{1,0:T(8,128)(2,1)} %bitcast.89), kind=kOutput, calls=%fused_computation.93 | convolution fusion | flops 8589934592 | bytes 27262976 | tf_op jit(solution)/shard_map/dot_general | solution.py:391
  209.1 0.9 slice.76
  210.1 0.3 copy.140
  210.5 0.3 copy.139
  210.8 1.4 subtract_convert_fusion
  212.2 0.5 fusion.44
  212.7 0.1 copy.120
  212.8 0.2 fusion.20
  213.0 0.1 copy.121
  213.1 0.1 copy.123
  213.2 0.2 fusion.32
  213.4 0.3 fusion.6
  213.7 0.6 copy.168
  214.3 69.1 %tail.1 = bf16[16,512]{1,0:T(8,128)(2,1)} custom-call(bf16[16,256]{1,0:T(8,128)(2,1)} %bitcast.103, bf16[16,512]{1,0:T(8,128)(2,1)} %bitcast.101, f32[16,1,512]{2,1,0:T(1,128)} %bitcast.100, bf16[256,8192]{1,0:T(8,128)(2,1)} %wo_hbm.1, bf16[8192,256]{1,0:T(8,128)(2,1)} %bitcast.91, bf16[128,8192]{1,0:T(8,128)(2,1)} %wd_hbm.1), custom_call_target="tpu_custom_call" | custom-call | tf_op jit(solution)/shard_map/tail/pallas_call | solution.py:239
  283.4 1.3 copy.170
  (45 shorter events, 1.1 us)
Async XLA Ops:
  6.5 9.7 %copy-start.2 = (bf16[2,8192]{1,0:T(2,128)(2,1)S(1)}, bf16[2,8192]{1,0:T(2,128)(2,1)}, u32[]{:S(2)}) copy-start(bf16[2,8192]{1,0:T(2,128)(2,1)} %param.18) | copy-start | bytes 98308
  11.6 20.5 %all-to-all-start = ((bf16[8,2,64,512]{3,2,1,0:T(8,128)(2,1)}), bf16[8,2,64,512]{3,2,1,0:T(8,128)(2,1)S(1)}, u32[]{:S(2)}, u32[]{:S(2)}) async-start(bf16[8,2,64,512]{3,2,1,0:T(8,128)(2,1)} %copy.105), calls=%async_computation | async-start | bytes 2097152 | tf_op jit(solution)/shard_map/all_to_all | solution.py:387
  16.2 175.7 %all-gather.2.cloned.1.call-start = ((), (), s32[]{:S(2)}) async-start(), calls=%async_computation.1 | async-start | bytes 17825792 | tf_op jit(solution)/shard_map/all_gather | solution.py:392
  75.5 8.1 %copy-start.4 = (s32[64]{0:T(128)S(1)}, s32[64]{0:T(128)}, u32[]{:S(2)}) copy-start(s32[64]{0:T(128)} %param.14) | copy-start | bytes 772
  75.5 8.1 %copy-start.5 = (s32[64]{0:T(128)S(1)}, s32[64]{0:T(128)}, u32[]{:S(2)}) copy-start(s32[64]{0:T(128)} %param.15) | copy-start | bytes 772
  95.5 7.0 %copy-start.3 = (bf16[2,8,512]{2,1,0:T(8,128)(2,1)S(1)}, bf16[2,8,512]{2,1,0:T(8,128)(2,1)}, u32[]{:S(2)}) copy-start(bf16[2,8,512]{2,1,0:T(8,128)(2,1)} %param.17) | copy-start | bytes 49156
  95.5 28.5 %copy-start.6 = (s32[8]{0:T(128)S(1)}, s32[8]{0:T(128)}, u32[]{:S(2)}) copy-start(s32[8]{0:T(128)} %param.16) | copy-start | bytes 100
  124.2 6.0 %copy-start = (bf16[256,8192]{1,0:T(8,128)(2,1)S(1)}, bf16[256,8192]{1,0:T(8,128)(2,1)}, u32[]{:S(2)}) copy-start(bf16[256,8192]{1,0:T(8,128)(2,1)} %copy.136) | copy-start | bytes 12582916
  210.8 2.6 copy-start.1
Sparse Core Ops, SparseCore 0:
  75.6 116.2 all-gather.1

commit v2 on v1

v2 whole, which is shorter than its diff:
```python
import math

import jax
import jax.numpy as jnp
import numpy as np
from jax import lax
from jax.experimental import pallas as pl
from jax.experimental.pallas import tpu as pltpu
from jax.sharding import PartitionSpec as P

D = 8192
HD = 128
C = 64
CD = 8
EPS = 1e-05
THETA = 10000.0
MASKED = -1e30
SCALE = 1.0 / math.sqrt(HD)
MESH = pl.DeviceIdType.MESH
BF = jnp.bfloat16
F32 = jnp.float32


def fold_squares(part):
    sq = part * part
    return (sq[:, 0:128] + sq[:, 128:256]) + (sq[:, 256:384] + sq[:, 384:512])


def rotate(vectors, cosine, sine):
    return vectors * cosine + pltpu.roll(vectors, 64, 1) * sine


ORDER = (
    (-1, 0), (1, 0), (0, -1), (0, 1), (2, 0), (-1, -1), (-1, 1), (1, -1), (1, 1), (0, 2),
    (2, -1), (2, 1), (-1, 2), (1, 2), (2, 2),
)


def layer_kernel(
    x_ref, tok_ref, gain_ref, rep_kv_ref, rep_gu_ref, sel_ref, match_ref, pos_ref, cosk_ref, sink_ref, cosq_ref, sinq_ref,
    plen_ref, wq_hbm, wkv_hbm, wo_hbm, wgu_hbm, wd_hbm, out_ref,
    wq, raw, wkv, wo, wgu, wd, pick_kv, pick_gu, spans, kv_acc, span_ss, toks, queries, partials, fresh,
    send_a, recv_a, rows, own_terms, send_d1, recv_d1, send_d2, recv_d2, send_d3, recv_d3, res,
    wsem, gsem, sx, rx, st, rt, sq, rq, sp, rp,
    sa, ra, s1, r1, s2, r2, s3, r3, sd1, rd1, sd2, rd2, sd3, rd3,
):
    s = lax.axis_index("seq")
    h = lax.axis_index("head")
    y = s // 2
    c = lax.rem(s, 2)
    slot = c * 4 + y
    pair = s + 1 - 2 * c
    px = h // 4
    pz = lax.rem(h, 4)

    def at_head(k):
        return lax.rem(h + k, 16)

    def at_seq(k):
        return lax.rem(s + k, 8)

    barrier = pltpu.get_barrier_semaphore()

    @pl.loop(1, 16)
    def _(k):
        pl.semaphore_signal(barrier, inc=1, device_id=(s, at_head(k)), device_id_type=MESH)

    @pl.loop(1, 8)
    def _(k):
        pl.semaphore_signal(barrier, inc=1, device_id=(at_seq(k), h), device_id_type=MESH)

    def weight_copy(which, j):
        cols = pl.ds(pl.multiple_of(j * 512, 512), 512)
        if which == 0:
            return pltpu.make_async_copy(wkv_hbm.at[pl.ds(pl.multiple_of(j * 2048, 2048), 2048)], raw.at[j], wsem.at[0, j])
        if which == 1:
            return pltpu.make_async_copy(wq_hbm.at[cols], wq.at[j], wsem.at[1, j])
        if which == 2:
            return pltpu.make_async_copy(wo_hbm.at[:, cols], wo.at[j], wsem.at[2, j])
        return pltpu.make_async_copy(wd_hbm.at[:, cols], wd.at[j], wsem.at[3, j])

    def gate_up_copy(j):
        return pltpu.make_async_copy(
            wgu_hbm.at[pl.ds(pl.multiple_of(j * 1024, 1024), 1024)], raw.at[j, pl.ds(0, 1024)], gsem.at[j]
        )

    for which in range(4):
        @pl.loop(0, 16)
        def _(j):
            weight_copy(which, j).start()

    def remote(src, dst, ssem, rsem, device):
        return pltpu.make_async_remote_copy(
            src_ref=src, dst_ref=dst, send_sem=ssem, recv_sem=rsem, device_id=device, device_id_type=MESH
        )

    row = lax.broadcasted_iota(jnp.int32, (256, 256), 0)
    col = lax.broadcasted_iota(jnp.int32, (256, 256), 1)
    low = lax.rem(col, 4)
    pick_kv[...] = jnp.where(row == (lax.rem(low, 2) * 2 + low // 2) * 64 + col // 4, 1.0, 0.0).astype(F32)
    pick_gu[...] = jnp.where(row == lax.rem(col, 2) * 128 + col // 2, 1.0, 0.0).astype(F32)

    spans[h] = x_ref[...]
    toks[h] = tok_ref[...]
    queries[s, 16:32] = plen_ref[...]
    kv_acc[...] = jnp.zeros_like(kv_acc)
    span_ss[...] = jnp.zeros_like(span_ss)

    pl.semaphore_wait(barrier, 22)

    def copy_t(k):
        t = at_head(k)
        return remote(toks.at[h], toks.at[h], st.at[t], rt.at[h], (s, t))

    def came_t(k):
        f = at_head(16 - k)
        return remote(toks.at[f], toks.at[f], st.at[f], rt.at[f], (s, f))

    @pl.loop(1, 16)
    def _(k):
        copy_t(k).start()

    def place(half, a, b):
        dx, dz = (a, b) if half == 0 else (b, a)
        return lax.rem(px + dx + 4, 4) * 4 + lax.rem(pz + dz + 4, 4)

    sends = []

    def push(half, block, part, axis, way):
        there = place(half, way, 0) if axis == 0 else place(half, 0, way)
        first, size, sem = ((0, 128, 0), (128, 128, 1), (0, 256, 0))[part]
        where = spans.at[block, pl.ds(half * 256 + first, size)]
        copy = remote(where, where, sx.at[len(sends)], rx.at[block, half * 2 + sem], (s, there))
        copy.start()
        sends.append(copy)

    def wait_for(half, block, part):
        first, size, sem = ((0, 128, 0), (128, 128, 1), (0, 256, 0))[part]
        where = spans.at[block, pl.ds(half * 256 + first, size)]
        remote(where, where, sx.at[0], rx.at[block, half * 2 + sem], (s, h)).wait_recv()

    def unpack(block):
        weight_copy(0, block).wait()

        @pl.loop(0, 8)
        def _(b):
            pick = (pick_kv[...] * rep_kv_ref[block * 8 + b]).astype(BF)
            part = raw[block, pl.ds(pl.multiple_of(b * 256, 256), 256)]
            got = jnp.dot(pick, part, preferred_element_type=F32).astype(BF)
            at = pl.ds(pl.multiple_of(b * 64, 64), 64)
            for i in range(4):
                wkv[block, at, pl.ds(i * 128, 128)] = got[i * 64:(i + 1) * 64]

    def take(half, block):
        @pl.loop(0, 2)
        def _(i):
            at = pl.ds(pl.multiple_of(half * 256 + i * 128, 128), 128)
            part = spans[block, at]
            span_ss[at] += fold_squares(part.astype(F32))
            kv_acc[at] += jnp.dot(part, wkv[block], preferred_element_type=F32)

    for half in range(2):
        for way in (1, -1):
            push(half, h, 2, 0, way)
    for half in range(2):
        for way in (1, -1):
            push(half, h, 2, 1, way)

    unpack(h)
    for half in range(2):
        take(half, h)

    def project_queries():
        @pl.loop(0, 16)
        def _(j):
            weight_copy(1, j).wait()

        @pl.loop(1, 16)
        def _(k):
            came_t(k).wait_recv()

        def body(j, carry):
            acc, ss = carry
            part = toks[j].astype(F32)
            scaled = (part * gain_ref[j]).astype(BF)
            return acc + jnp.dot(scaled, wq[j], preferred_element_type=F32), ss + fold_squares(part)

        acc, ss = lax.fori_loop(0, 16, body, (jnp.zeros((16, 256), F32), jnp.zeros((16, 128), F32)))
        scale = lax.rsqrt(jnp.sum(ss, axis=1, keepdims=True) / D + EPS)
        for j in range(2):
            at = slice(j * 128, (j + 1) * 128)
            queries[s, 0:16, at] = rotate(acc[:, at] * scale, cosq_ref[...], sinq_ref[...]).astype(BF)

        @pl.loop(1, 8)
        def _(k):
            copy_q(k).start()

        return scale

    def copy_q(k):
        t = at_seq(k)
        return remote(queries.at[s], queries.at[s], sq.at[t], rq.at[s], (t, h))

    def came_q(k):
        f = at_seq(8 - k)
        return remote(queries.at[f], queries.at[f], sq.at[f], rq.at[f], (f, h))

    unpacked = set()
    token_scale = None
    for number, (a, b) in enumerate(ORDER):
        blocks = [place(half, a, b) for half in range(2)]
        for half in range(2):
            block = blocks[half]
            parts = (0, 1) if (a == 2 and b == 0) or b == 2 else (2,)
            for part in parts:
                wait_for(half, block, part)
            if b == 0:
                if a == -1:
                    push(half, block, 0, 0, 1)
                if a == 1:
                    push(half, block, 1, 0, -1)
                push(half, block, 2, 1, 1)
                push(half, block, 2, 1, -1)
            elif b == -1:
                push(half, block, 0, 1, 1)
            elif b == 1:
                push(half, block, 1, 1, -1)
        for half in range(2):
            source = (a % 4, b % 4) if half == 0 else (b % 4, a % 4)
            if source not in unpacked:
                unpacked.add(source)
                unpack(blocks[half])
            take(half, blocks[half])
        if number == 3:
            token_scale = project_queries()

    @pl.loop(0, 16)
    def _(j):
        gate_up_copy(j).start()

    def project_fresh(j, acc):
        return acc + jnp.dot(toks[j], wkv[j], preferred_element_type=F32)

    new_kv = lax.fori_loop(0, 16, project_fresh, jnp.zeros((16, 512), F32)) * token_scale

    @pl.loop(1, 8)
    def _(k):
        came_q(k).wait_recv()

    chosen = jnp.dot(sel_ref[...], queries[...].reshape(256, 256), preferred_element_type=F32)
    length = chosen[16:24, 0:1] * 128.0 + chosen[24:32, 0:1]
    length = jnp.concatenate([length, length], axis=0)
    token_span = lax.broadcasted_iota(jnp.int32, (16, 512), 1) // C
    row_span = lax.rem(lax.broadcasted_iota(jnp.int32, (16, 512), 0), CD)
    live = (token_span == row_span) & (pos_ref[...] < length)
    span_scale = lax.rsqrt(jnp.sum(span_ss[...], axis=1, keepdims=True) / D + EPS)
    lanes = lax.broadcasted_iota(jnp.int32, (16, 128), 1)
    for j in range(2):
        at = slice(j * 128, (j + 1) * 128)
        keys = rotate(kv_acc[:, at] * span_scale, cosk_ref[...], sink_ref[...]).astype(BF)
        values = (kv_acc[:, 256 + j * 128:384 + j * 128] * span_scale).astype(BF)
        scores = lax.dot_general(
            chosen[0:16, at].astype(BF), keys, (((1,), (1,)), ((), ())), preferred_element_type=F32
        ) * SCALE
        scores = jnp.where(live, scores, MASKED)
        top = jnp.max(scores, axis=1, keepdims=True)
        weights = jnp.where(live, jnp.exp(scores - top), 0.0)
        total = jnp.sum(weights, axis=1, keepdims=True)
        partials[s, j * 16:(j + 1) * 16, 0:128] = jnp.dot(weights.astype(BF), values, preferred_element_type=F32)
        partials[s, j * 16:(j + 1) * 16, 128:256] = jnp.where(lanes < 64, top, total)

    def copy_p(k):
        t = at_seq(k)
        return remote(partials.at[s], partials.at[s], sp.at[t], rp.at[s], (t, h))

    def came_p(k):
        f = at_seq(8 - k)
        return remote(partials.at[f], partials.at[f], sp.at[f], rp.at[f], (f, h))

    @pl.loop(1, 8)
    def _(k):
        copy_p(k).start()

    for j in range(2):
        at = slice(j * 128, (j + 1) * 128)
        fresh[j] = rotate(new_kv[:, at], cosq_ref[...], sinq_ref[...]).astype(BF).astype(F32)
        fresh[2 + j] = new_kv[:, 256 + j * 128:384 + j * 128].astype(BF).astype(F32)

    @pl.loop(0, 16)
    def _(j):
        gate_up_copy(j).wait()

        @pl.loop(0, 4)
        def _(b):
            pick = (pick_gu[...] * rep_gu_ref[j * 4 + b]).astype(BF)
            part = raw[j, pl.ds(pl.multiple_of(b * 256, 256), 256)]
            got = jnp.dot(pick, part, preferred_element_type=F32).astype(BF)
            at = pl.ds(pl.multiple_of(b * 128, 128), 128)
            wgu[j, at, 0:128] = got[0:128]
            wgu[j, at, 128:256] = got[128:256]

    @pl.loop(1, 8)
    def _(k):
        came_p(k).wait_recv()

    match = match_ref[...] > 0.0
    own_q = queries[s, 0:16].astype(F32)
    heads = []
    for j in range(2):
        steps = []
        for t in range(2):
            block = partials[:, pl.ds(j * 16 + t * 8, 8), :].reshape(64, 256)
            stats = block[:, 128:256].T
            tops, sums = stats[0:8], stats[64:72]
            q = own_q[t * 8:(t + 1) * 8, j * 128:(j + 1) * 128]
            fresh_scores = [
                jnp.sum(q * fresh[j, u * 8:(u + 1) * 8], axis=1, keepdims=True) * SCALE for u in range(t + 1)
            ]
            best = jnp.max(jnp.where(match, tops, MASKED), axis=1, keepdims=True)
            for score in fresh_scores:
                best = jnp.maximum(best, score)
            factor = jnp.where(match, jnp.exp(jnp.where(match, tops, best) - best), 0.0)
            total = jnp.sum(factor * sums, axis=1, keepdims=True)
            value = jnp.dot(factor, block[:, 0:128], precision=lax.Precision.HIGHEST, preferred_element_type=F32)
            for u, score in enumerate(fresh_scores):
                e = jnp.exp(score - best)
                total = total + e
                value = value + e * fresh[2 + j, u * 8:(u + 1) * 8]
            steps.append(value / total)
        heads.append(jnp.concatenate(steps, axis=0))
    att = jnp.concatenate(heads, axis=1).astype(BF)

    @pl.loop(0, 16)
    def _(j):
        weight_copy(2, j).wait()

    def copy_a(k):
        t = at_head(k)
        return remote(send_a.at[t], recv_a.at[h], sa.at[t], ra.at[h], (s, t))

    def came_a(k):
        f = at_head(16 - k)
        return remote(send_a.at[f], recv_a.at[f], sa.at[f], ra.at[f], (s, f))

    @pl.loop(1, 16)
    def _(k):
        t = at_head(k)
        send_a[t] = jnp.dot(att, wo[t], preferred_element_type=F32).astype(BF)
        copy_a(k).start()

    res[...] = tok_ref[...].astype(F32) + jnp.dot(att, wo[h], preferred_element_type=F32)

    @pl.loop(1, 16)
    def _(k):
        came_a(k).wait_recv()
        res[...] += recv_a[at_head(16 - k)].astype(F32)

    rows[h, slot] = res[...].astype(BF)

    def copy_1(k):
        t = lax.rem(s + k, 8)
        return remote(rows.at[h, slot], rows.at[h, slot], s1.at[t], r1.at[s], (t, h))

    def came_1(k):
        f = lax.rem(s + 8 - k, 8)
        place = lax.rem(f, 2) * 4 + f // 2
        return remote(rows.at[h, place], rows.at[h, place], s1.at[f], r1.at[f], (f, h))

    @pl.loop(1, 8)
    def _(k):
        copy_1(k).start()

    @pl.loop(1, 8)
    def _(k):
        came_1(k).wait_recv()

    mine = pl.ds(c * 4, 4)
    other = pl.ds(4 - c * 4, 4)

    def copy_2(k):
        t = at_head(k)
        return remote(rows.at[h, mine], rows.at[h, mine], s2.at[t], r2.at[h], (s, t))

    def came_2(k):
        f = at_head(16 - k)
        return remote(rows.at[f, mine], rows.at[f, mine], s2.at[f], r2.at[f], (s, f))

    def copy_3(k):
        f = at_head(16 - k)
        return remote(rows.at[f, mine], rows.at[f, mine], s3.at[f], r3.at[f], (pair, h))

    def came_3(k):
        f = at_head(16 - k)
        return remote(rows.at[f, other], rows.at[f, other], s3.at[f], r3.at[f], (pair, h))

    @pl.loop(1, 16)
    def _(k):
        copy_2(k).start()

    @pl.loop(0, 16)
    def _(j):
        weight_copy(3, j).wait()

    def block(j, carry):
        acc, squares = carry
        part = rows[j].reshape(128, 512)
        squares = squares + fold_squares(part.astype(F32))
        return acc + jnp.dot(part, wgu[j], preferred_element_type=F32), squares

    carry = block(h, (jnp.zeros((128, 256), F32), jnp.zeros((128, 128), F32)))

    def step(k, carry):
        came_2(k).wait_recv()
        copy_3(k).start()
        came_3(k).wait_recv()
        return block(at_head(16 - k), carry)

    acc, squares = lax.fori_loop(1, 16, step, carry)
    scale = lax.rsqrt(jnp.sum(squares, axis=1, keepdims=True) / D + EPS)
    gate = acc[:, 0:128] * scale
    up = acc[:, 128:256] * scale
    act = (gate / (1.0 + jnp.exp(-gate)) * up).astype(BF)

    def copy_d1(t):
        return remote(send_d1.at[t], recv_d1.at[t], sd1.at[t], rd1.at[t], (pair, h))

    def copy_d2(t):
        return remote(send_d2.at[t], recv_d2.at[h], sd2.at[t], rd2.at[h], (s, t))

    def came_d2(f):
        return remote(send_d2.at[f], recv_d2.at[f], sd2.at[f], rd2.at[f], (s, f))

    @pl.loop(0, 16)
    def _(k):
        t = at_head(k + 1)
        terms = jnp.dot(act, wd[t], preferred_element_type=F32)
        low, high = terms[0:64], terms[64:128]
        own_terms[t] = jnp.where(c == 0, low, high)
        send_d1[t] = jnp.where(c == 0, high, low).astype(BF)
        copy_d1(t).start()

    @pl.loop(0, 15)
    def _(k):
        t = at_head(k + 1)
        copy_d1(t).wait_recv()
        send_d2[t] = (own_terms[t] + recv_d1[t].astype(F32)).astype(BF)
        copy_d2(t).start()

    copy_d1(h).wait_recv()
    own_terms[h] = own_terms[h] + recv_d1[h].astype(F32)

    @pl.loop(1, 16)
    def _(k):
        f = at_head(16 - k)
        came_d2(f).wait_recv()
        own_terms[h] += recv_d2[f].astype(F32)

    def copy_d3(k):
        t = lax.rem(y + k, 4)
        return remote(send_d3.at[t], recv_d3.at[y], sd3.at[t], rd3.at[y], (t * 2 + c, h))

    def came_d3(k):
        f = lax.rem(y + 4 - k, 4)
        return remote(send_d3.at[f], recv_d3.at[f], sd3.at[f], rd3.at[f], (f * 2 + c, h))

    send_d3[...] = own_terms[h].reshape(4, 16, 512).astype(BF)
    for k in range(1, 4):
        copy_d3(k).start()
    total = res[...] + own_terms[h, pl.ds(pl.multiple_of(y * 16, 16), 16)]
    for k in range(1, 4):
        came_d3(k).wait_recv()
        total = total + recv_d3[lax.rem(y + 4 - k, 4)].astype(F32)
    out_ref[...] = total.astype(BF)

    for copy in sends:
        copy.wait_send()

    @pl.loop(1, 16)
    def _(k):
        copy_t(k).wait_send()
        copy_a(k).wait_send()
        copy_2(k).wait_send()
        copy_3(k).wait_send()
        copy_d1(at_head(k)).wait_send()
        copy_d2(at_head(k)).wait_send()

    copy_d1(h).wait_send()

    @pl.loop(1, 8)
    def _(k):
        copy_1(k).wait_send()
        copy_q(k).wait_send()
        copy_p(k).wait_send()

    for k in range(1, 4):
        copy_d3(k).wait_send()


def local(
    hidden_states, span_group, span_slot, span_block, prompt_len, new_tokens, norm_gain, w_q, w_kv, w_o, w_gate_up, w_down
):
    s = lax.axis_index("seq")
    gains = norm_gain.astype(F32)
    freqs = jnp.exp(jnp.arange(HD // 2).astype(F32) * (-2.0 * math.log(THETA) / HD))
    my_group = lax.dynamic_slice_in_dim(span_group[:, 0], s * CD, CD)
    my_slot = lax.dynamic_slice_in_dim(span_slot, s * CD, CD)
    my_block = lax.dynamic_slice_in_dim(span_block, s * CD, CD)
    base = (my_block * C).astype(F32)[:, None] * freqs
    step = jnp.asarray(np.arange(C), F32)[:, None] * freqs
    base_cos, base_sin = jnp.cos(base)[:, None], jnp.sin(base)[:, None]
    step_cos, step_sin = jnp.cos(step)[None], jnp.sin(step)[None]
    cos_k = (base_cos * step_cos - base_sin * step_sin).reshape(CD * C, HD // 2)
    sin_k = (base_sin * step_cos + base_cos * step_sin).reshape(CD * C, HD // 2)
    positions = prompt_len[None, :] + jnp.arange(2, dtype=jnp.int32)[:, None]
    angles = positions.reshape(16).astype(F32)[:, None] * freqs
    cos_q, sin_q = jnp.cos(angles), jnp.sin(angles)
    offsets = (my_block[:, None] * C + jnp.arange(C)).reshape(1, CD * C).astype(F32)
    wanted = (my_group * 32 + my_slot)[None, :] + jnp.arange(4)[:, None] * 8
    sel = (wanted.reshape(32, 1) == jnp.arange(256)[None, :]).astype(BF)
    owner = span_group[:, 0] * 8 + span_slot
    match = (owner[None, :] == (s * 8 + jnp.arange(8))[:, None]).astype(F32)
    lengths = jnp.concatenate([prompt_len // 128, prompt_len % 128]).astype(BF)
    rep_kv = jnp.broadcast_to(gains[0][:, None], (D, 4)).reshape(128, 1, 256)
    rep_gu = jnp.broadcast_to(gains[1][:, None], (D, 2)).reshape(64, 1, 256)
    packed_kv = w_kv.reshape(D, 2, 2, HD).transpose(0, 2, 1, 3).reshape(D * 4, HD)

    vmem = pl.BlockSpec(memory_space=pltpu.VMEM)
    hbm = pl.BlockSpec(memory_space=pl.ANY)
    dma = pltpu.SemaphoreType.DMA
    out = pl.pallas_call(
        layer_kernel,
        name="layer",
        out_shape=jax.ShapeDtypeStruct((16, 512), BF),
        in_specs=[vmem] * 13 + [hbm] * 5,
        out_specs=vmem,
        scratch_shapes=[
            pltpu.VMEM((16, 512, 256), BF),
            pltpu.VMEM((16, 2048, 128), BF),
            pltpu.VMEM((16, 512, 512), BF),
            pltpu.VMEM((16, 256, 512), BF),
            pltpu.VMEM((16, 512, 256), BF),
            pltpu.VMEM((16, 128, 512), BF),
            pltpu.VMEM((256, 256), F32),
            pltpu.VMEM((256, 256), F32),
            pltpu.VMEM((16, 512, 512), BF),
            pltpu.VMEM((512, 512), F32),
            pltpu.VMEM((512, 128), F32),
            pltpu.VMEM((16, 16, 512), BF),
            pltpu.VMEM((8, 32, 256), BF),
            pltpu.VMEM((8, 32, 256), F32),
            pltpu.VMEM((4, 16, 128), F32),
            pltpu.VMEM((16, 16, 512), BF),
            pltpu.VMEM((16, 16, 512), BF),
            pltpu.VMEM((16, 8, 16, 512), BF),
            pltpu.VMEM((16, 64, 512), F32),
            pltpu.VMEM((16, 64, 512), BF),
            pltpu.VMEM((16, 64, 512), BF),
            pltpu.VMEM((16, 64, 512), BF),
            pltpu.VMEM((16, 64, 512), BF),
            pltpu.VMEM((4, 16, 512), BF),
            pltpu.VMEM((4, 16, 512), BF),
            pltpu.VMEM((16, 512), F32),
            dma((4, 16)), dma((16,)), dma((48,)), dma((16, 4)), dma((16,)), dma((16,)), dma((8,)), dma((8,)), dma((8,)), dma((8,)),
            dma((16,)), dma((16,)), dma((8,)), dma((8,)), dma((16,)), dma((16,)), dma((16,)), dma((16,)),
            dma((16,)), dma((16,)), dma((16,)), dma((16,)), dma((4,)), dma((4,)),
        ],
        compiler_params=pltpu.CompilerParams(
            collective_id=1, has_side_effects=True, vmem_limit_bytes=60 * 2**20
        ),
    )(
        hidden_states.reshape(CD * C, 512),
        new_tokens.reshape(16, 512),
        gains[0].reshape(16, 1, 512),
        rep_kv,
        rep_gu,
        sel,
        match,
        offsets,
        jnp.concatenate([cos_k, cos_k], axis=1),
        jnp.concatenate([-sin_k, sin_k], axis=1),
        jnp.concatenate([cos_q, cos_q], axis=1),
        jnp.concatenate([-sin_q, sin_q], axis=1),
        jnp.broadcast_to(lengths[:, None], (16, 256)),
        w_q,
        packed_kv,
        w_o,
        w_gate_up.reshape(D * 2, HD),
        w_down,
    )
    return out.reshape(2, 8, 512)


def solution(mesh):
    placed = (
        P("seq", None, "head"),
        P(),
        P(),
        P(),
        P("seq"),
        P(None, "seq", "head"),
        P(),
        P(None, "head"),
        P(None, None, "head"),
        P("head", None),
        P(None, None, ("seq", "head")),
        P(("seq", "head"), None),
    )
    return jax.shard_map(
        local, mesh=mesh, in_specs=placed, out_specs=P(None, "seq", "head"), check_vma=False
    )
```

time: 294 us -> 163 us (0.55)
  Pallas kernels: 69.1 us -> 148 us
  waiting for transfers between devices: 67.6 us -> 0 us
  blocking collectives: 63 us -> 0 us
  local copies, waits for them, and re-layouts: 38 us -> 6.15 us
  matrix products: 27 us -> 0 us
  between operations: 13.6 us -> 0.08 us
  starting transfers between devices: 4.59 us -> 0 us
    pallas_call x1, Pallas kernels: 69.1 us -> 148 us  [local(): pl.pallas_call(layer_kernel, name='layer', out_shape=jax.ShapeDtypeStruct...]
    all_gather x1 -> x0, waiting for transfers between devices: 52.3 us -> none  [local(): lax.all_gather(normed_rows, 'head', axis=1, tiled=True)]
    psum x1 -> x0, blocking collectives: 41.7 us -> none  [local(): squares = lax.psum(jnp.sum(arrived_float * arrived_float, axis=1), 'head')]
    dot_general x8 -> x0, matrix products: 27 us -> none  [the longest x1 17.2 us: local(): jnp.dot(lax.all_gather(normed_rows, 'head', axis=1, tiled=True), kv_flat,...]
    all_gather x1 -> x0, blocking collectives: 21.3 us -> none  [local(): token_full = lax.all_gather(new_tokens, 'head', axis=2, tiled=True)]
    dot_general x2 -> x0, local copies, waits for them, and re-layouts: 17.8 us -> none  [the longest x1 11.4 us: local(): jnp.dot(flat_tokens, kv_flat, preferred_element_type=jnp.float32)]
    all_to_all x1 -> x0, waiting for transfers between devices: 15.3 us -> none  [local(): lax.all_to_all(packed, 'seq', split_axis=0, concat_axis=0, tiled=True)]
    unnamed x20 -> x1, local copies, waits for them, and re-layouts: 15.3 us -> 1.32 us
  transfers between devices with their start and end apart: 2 -> 0, of which waited for: 2 -> 0; matrix products, arithmetic and copies ran while one was open for 15% -> 0% of each run, Pallas kernels for 0% -> 0%
where the time goes in v2:
time: 163 us; the launch traced here: 162 us
  Pallas kernels  148 us (91%)
  other arithmetic  7.94 us (5%)
  local copies, waits for them, and re-layouts  6.15 us (4%)
    pallas_call x1, Pallas kernels, local(): pl.pallas_call(layer_kernel, name='layer', out_shape=jax.ShapeDtypeStruct...  148 us

profile of v2, /device:TPU:0, one launch (start us, length us, event | category | flops | bytes accessed | tf_op | source)
XLA Modules:
  0.0 161.9 jit_solution(8957342205542974448)
XLA Ops:
  0.0 0.8 fusion.6
  0.8 0.1 multiply_cosine_fusion.1
  0.9 0.1 fusion.1
  1.0 0.1 multiply_add_fusion
  1.1 0.8 pad_maximum_fusion.1.sink_ref
  2.0 0.8 pad_maximum_fusion.cosk_ref
  2.8 0.7 add_convert_fusion.1
  3.5 0.1 convert_element_type.51
  3.6 0.1 fusion.3
  3.7 0.7 pad_maximum_fusion.2
  4.4 0.1 broadcast_add_fusion
  4.4 0.1 add.101
  4.5 0.7 fusion.2.sel_ref
  5.2 0.1 add_convert_fusion
  5.3 0.7 convert_element_type.47.pos_ref
  6.0 0.7 bitcast_add_fusion
  6.6 0.7 compare_convert_fusion.match_ref
  7.3 0.7 fusion.5
  8.0 0.1 pad_maximum_fusion.4
  8.0 0.7 broadcast_in_dim.20.plen_ref
  8.7 1.5 fusion.7
  10.2 0.1 copy.16
  10.3 0.7 copy.19.rep_gu_ref
  11.0 0.8 convert_element_type.43
  11.8 0.1 slice_reduce_fusion
  11.9 0.1 broadcast_in_dim.14
  12.0 0.1 copy.15
  12.1 0.7 copy.18.rep_kv_ref
  12.8 147.7 %layer.1 = bf16[16,512]{1,0:T(8,128)(2,1)} custom-call(bf16[512,512]{1,0:T(8,128)(2,1)} %bitcast.24, bf16[16,512]{1,0:T(8,128)(2,1)} %bitcast.30, f32[16,1,512]{2,1,0:T(1,128)} %bitcast.27, f32[128,1,256]{2,1,0:T(1,128)} %copy.18.rep_kv_ref, f32[64,1,256]{2,1,0:T(1,128)} %copy.19.rep_gu_ref, bf16[32,256]{1,0:T(8,128)(2,1)} %fusion.2.sel_ref, ...), custom_call_target="tpu_custom_call" | custom-call | tf_op jit(solution)/shard_map/layer/pallas_call | solution.py:530
  160.6 1.3 copy.21
  (6 shorter events, 0.1 us)

commit v3 on v2

v3 whole, which is shorter than its diff:
```python
import math

import jax
import jax.numpy as jnp
import numpy as np
from jax import lax
from jax.experimental import pallas as pl
from jax.experimental.pallas import tpu as pltpu
from jax.sharding import PartitionSpec as P

D = 8192
HD = 128
C = 64
CD = 8
EPS = 1e-05
THETA = 10000.0
MASKED = -1e30
SCALE = 1.0 / math.sqrt(HD)
MESH = pl.DeviceIdType.MESH
BF = jnp.bfloat16
F32 = jnp.float32


def fold_squares(part, weight):
    sq = part * part * weight
    return (sq[:, 0:128] + sq[:, 128:256]) + (sq[:, 256:384] + sq[:, 384:512])


def rotate(vectors, cosine, sine):
    return vectors * cosine + pltpu.roll(vectors, 64, 1) * sine


ORDER = (
    (-1, 0), (1, 0), (0, -1), (0, 1), (2, 0), (-1, -1), (1, 1), (-1, 1), (1, -1), (0, 2),
    (2, -1), (2, 1), (-1, 2), (1, 2), (2, 2),
)


def layer_kernel(
    x_ref, tok_ref, gain_ref, group_ref, slot_ref, block_ref, length_ref, freq_ref, step_ref, wq_hbm, wkv_hbm, wo_hbm, wgu_hbm, wd_hbm, out_ref,
    wq, raw, raw_gu, wkv, wo, wgu, wd, pick_kv, pick_gu, inv_gain, cosk, sink, cosq, sinq, spans, kv_acc, span_ss, toks, queries, partials, fresh,
    send_a, recv_a, rows, own_terms, send_d1, recv_d1, send_e, recv_e, send_f, recv_f, send_d3, recv_d3, res,
    gu_acc, row_ss,
    wsem, gsem, sx, rx, st, rt, sq, rq, sp, rp,
    sa, ra, s1, r1, s2, r2, s3, r3, sd1, rd1, se, re, sf, rf, sd3, rd3,
):
    s = lax.axis_index("seq")
    h = lax.axis_index("head")
    y = s // 2
    c = lax.rem(s, 2)
    slot = c * 4 + y
    pair = s + 1 - 2 * c
    px = h // 4
    pz = lax.rem(h, 4)

    def at_head(k):
        return lax.rem(h + k, 16)

    def at_seq(k):
        return lax.rem(s + k, 8)

    barrier = pltpu.get_barrier_semaphore()

    @pl.loop(1, 16)
    def _(k):
        pl.semaphore_signal(barrier, inc=1, device_id=(s, at_head(k)), device_id_type=MESH)

    @pl.loop(1, 8)
    def _(k):
        pl.semaphore_signal(barrier, inc=1, device_id=(at_seq(k), h), device_id_type=MESH)

    def weight_copy(which, j):
        cols = pl.ds(pl.multiple_of(j * 512, 512), 512)
        if which == 0:
            return pltpu.make_async_copy(wkv_hbm.at[pl.ds(pl.multiple_of(j * 2048, 2048), 2048)], raw.at[j], wsem.at[0, j])
        if which == 1:
            return pltpu.make_async_copy(wq_hbm.at[cols], wq.at[j], wsem.at[1, j])
        if which == 2:
            return pltpu.make_async_copy(wo_hbm.at[:, cols], wo.at[j], wsem.at[2, j])
        return pltpu.make_async_copy(wd_hbm.at[:, cols], wd.at[j], wsem.at[3, j])

    def gate_up_copy(j):
        return pltpu.make_async_copy(
            wgu_hbm.at[pl.ds(pl.multiple_of(j * 1024, 1024), 1024)], raw_gu.at[j], gsem.at[j]
        )

    for which in range(4):
        @pl.loop(0, 16)
        def _(j):
            weight_copy(which, j).start()

    @pl.loop(0, 16)
    def _(j):
        gate_up_copy(j).start()

    def remote(src, dst, ssem, rsem, device):
        return pltpu.make_async_remote_copy(
            src_ref=src, dst_ref=dst, send_sem=ssem, recv_sem=rsem, device_id=device, device_id_type=MESH
        )

    row = lax.broadcasted_iota(jnp.int32, (256, 256), 0)
    col = lax.broadcasted_iota(jnp.int32, (256, 256), 1)
    low = lax.rem(col, 4)
    pick_kv[...] = jnp.where(row == (lax.rem(low, 2) * 2 + low // 2) * 64 + col // 4, 1.0, 0.0).astype(BF)
    pick_gu[...] = jnp.where(row == lax.rem(col, 2) * 128 + col // 2, 1.0, 0.0).astype(BF)

    own_gain = gain_ref[:, pl.ds(pl.multiple_of(h * 512, 512), 512)].astype(F32)
    spans[h] = (x_ref[...].astype(F32) * own_gain[0:1]).astype(BF)
    toks[h] = (tok_ref[...].astype(F32) * own_gain[0:1]).astype(BF)

    def per_row(shape, values):
        rows_of = lax.rem(lax.broadcasted_iota(jnp.int32, shape, 0), 8)
        out = jnp.zeros(shape, jnp.int32)
        for i, value in enumerate(values):
            out = jnp.where(rows_of == i, value, out)
        return out

    lengths = per_row((8, 256), [length_ref[i] for i in range(8)])
    queries[s, 16:32] = jnp.concatenate([lengths // 128, lax.rem(lengths, 128)], axis=0).astype(F32).astype(BF)
    kv_acc[...] = jnp.zeros_like(kv_acc)
    span_ss[...] = jnp.zeros_like(span_ss)

    pl.semaphore_wait(barrier, 22)

    def make_tables():
        @pl.loop(0, 16)
        def _(j):
            g = gain_ref[:, pl.ds(pl.multiple_of(j * 512, 512), 512)].astype(F32)
            inv_gain[j] = 1.0 / (g * g)

        freq = freq_ref[...]
        sign = jnp.where(lax.broadcasted_iota(jnp.int32, (1, 128), 1) < 64, -1.0, 1.0).astype(F32)
        base = (per_row((8, 128), [block_ref[s * CD + i] for i in range(CD)]) * C).astype(F32) * freq
        base_cos, base_sin = jnp.cos(base), jnp.sin(base)
        step_cos, step_sin = step_ref[0], step_ref[1]
        for i in range(CD):
            bc, bs = base_cos[i:i + 1], base_sin[i:i + 1]
            cosk[i * C:(i + 1) * C] = bc * step_cos - bs * step_sin
            sink[i * C:(i + 1) * C] = (bs * step_cos + bc * step_sin) * sign
        later = lax.broadcasted_iota(jnp.int32, (16, 128), 0) // 8
        at = jnp.concatenate([lengths[:, 0:128], lengths[:, 0:128]], axis=0) + later
        angle = at.astype(F32) * freq
        cosq[...] = jnp.cos(angle)
        sinq[...] = jnp.sin(angle) * sign

    def copy_t(k):
        t = at_head(k)
        return remote(toks.at[h], toks.at[h], st.at[t], rt.at[h], (s, t))

    def came_t(k):
        f = at_head(16 - k)
        return remote(toks.at[f], toks.at[f], st.at[f], rt.at[f], (s, f))

    @pl.loop(1, 16)
    def _(k):
        copy_t(k).start()

    def place(half, a, b):
        dx, dz = (a, b) if half == 0 else (b, a)
        return lax.rem(px + dx + 4, 4) * 4 + lax.rem(pz + dz + 4, 4)

    sends = []

    def push(half, block, part, axis, way):
        there = place(half, way, 0) if axis == 0 else place(half, 0, way)
        first, size, sem = ((0, 128, 0), (128, 128, 1), (0, 256, 0))[part]
        where = spans.at[block, pl.ds(half * 256 + first, size)]
        copy = remote(where, where, sx.at[len(sends)], rx.at[block, half * 2 + sem], (s, there))
        copy.start()
        sends.append(copy)

    def wait_for(half, block, part):
        first, size, sem = ((0, 128, 0), (128, 128, 1), (0, 256, 0))[part]
        where = spans.at[block, pl.ds(half * 256 + first, size)]
        remote(where, where, sx.at[0], rx.at[block, half * 2 + sem], (s, h)).wait_recv()

    def unpack(block):
        weight_copy(0, block).wait()

        @pl.loop(0, 4)
        def _(b):
            part = raw[block, pl.ds(pl.multiple_of(b * 512, 512), 512)]
            part = jnp.concatenate([part[0:256], part[256:512]], axis=1)
            got = jnp.dot(pick_kv[...], part, preferred_element_type=F32).astype(BF)
            for i in range(4):
                for e in range(2):
                    at = pl.ds(pl.multiple_of(b * 128 + e * 64, 64), 64)
                    wkv[block, at, pl.ds(i * 128, 128)] = got[i * 64:(i + 1) * 64, e * 128:(e + 1) * 128]

    def unpack_gate_up(block):
        gate_up_copy(block).wait()

        @pl.loop(0, 2)
        def _(b):
            part = raw_gu[block, pl.ds(pl.multiple_of(b * 512, 512), 512)]
            part = jnp.concatenate([part[0:256], part[256:512]], axis=1)
            got = jnp.dot(pick_gu[...], part, preferred_element_type=F32).astype(BF)
            for i in range(2):
                for e in range(2):
                    at = pl.ds(pl.multiple_of(b * 256 + e * 128, 128), 128)
                    wgu[block, at, pl.ds(i * 128, 128)] = got[i * 128:(i + 1) * 128, e * 128:(e + 1) * 128]

    def take(block):
        @pl.loop(0, 2)
        def _(i):
            at = pl.ds(pl.multiple_of(i * 256, 256), 256)
            part = spans[block, at]
            span_ss[at] += fold_squares(part.astype(F32), inv_gain[block, 0:1])
            kv_acc[at] += jnp.dot(part, wkv[block], preferred_element_type=F32)

    for half in range(2):
        for way in (1, -1):
            push(half, h, 2, 0, way)
    for half in range(2):
        for way in (1, -1):
            push(half, h, 2, 1, way)

    make_tables()
    unpack(h)
    take(h)
    unpack_gate_up(15)

    def project_queries():
        @pl.loop(0, 16)
        def _(j):
            weight_copy(1, j).wait()

        @pl.loop(1, 16)
        def _(k):
            came_t(k).wait_recv()

        def body(j, carry):
            acc, ss = carry
            part = toks[j]
            ss = ss + fold_squares(part.astype(F32), inv_gain[j, 0:1])
            return acc + jnp.dot(part, wq[j], preferred_element_type=F32), ss

        acc, ss = lax.fori_loop(0, 16, body, (jnp.zeros((16, 256), F32), jnp.zeros((16, 128), F32)))
        scale = lax.rsqrt(jnp.sum(ss, axis=1, keepdims=True) / D + EPS)
        for j in range(2):
            at = slice(j * 128, (j + 1) * 128)
            queries[s, 0:16, at] = rotate(acc[:, at] * scale, cosq[...], sinq[...]).astype(BF)

        @pl.loop(1, 8)
        def _(k):
            copy_q(k).start()

        return scale

    def copy_q(k):
        t = at_seq(k)
        return remote(queries.at[s], queries.at[s], sq.at[t], rq.at[s], (t, h))

    def came_q(k):
        f = at_seq(8 - k)
        return remote(queries.at[f], queries.at[f], sq.at[f], rq.at[f], (f, h))

    arrived = [set(), set()]
    taken = {(0, 0)}
    token_scale = None
    for number, (a, b) in enumerate(ORDER):
        ready = sorted((arrived[0] & arrived[1]) - taken)
        for half in range(2):
            block = place(half, a, b)
            parts = (0, 1) if (a == 2 and b == 0) or b == 2 else (2,)
            for part in parts:
                wait_for(half, block, part)
            if b == 0:
                if a == -1:
                    push(half, block, 0, 0, 1)
                if a == 1:
                    push(half, block, 1, 0, -1)
                push(half, block, 2, 1, 1)
                push(half, block, 2, 1, -1)
            elif b == -1:
                push(half, block, 0, 1, 1)
            elif b == 1:
                push(half, block, 1, 1, -1)
            arrived[half].add((a % 4, b % 4) if half == 0 else (b % 4, a % 4))
        for source in ready[:2]:
            taken.add(source)
            unpack(place(0, *source))
            take(place(0, *source))
        unpack_gate_up(number)
        if number == 3:
            token_scale = project_queries()
    for source in sorted((arrived[0] & arrived[1]) - taken):
        unpack(place(0, *source))
        take(place(0, *source))

    lane = lax.broadcasted_iota(jnp.int32, (32, 256), 1)
    line = lax.broadcasted_iota(jnp.int32, (32, 256), 0)
    wanted = per_row((32, 256), [group_ref[s * CD + i] * 32 + slot_ref[s * CD + i] for i in range(CD)]) + line // 8 * 8
    sel = jnp.where(lane == wanted, 1.0, 0.0).astype(BF)
    lane = lax.broadcasted_iota(jnp.int32, (1, 512), 1)
    offset = lax.rem(lane, C)
    position = offset
    for i in range(CD):
        position = jnp.where(lane // C == i, block_ref[s * CD + i] * C + offset, position)
    position = position.astype(F32)
    lane = lax.broadcasted_iota(jnp.int32, (8, 64), 1)
    owner = jnp.zeros((8, 64), jnp.int32)
    for i in range(64):
        owner = jnp.where(lane == i, group_ref[i] * 8 + slot_ref[i], owner)
    match = owner == s * 8 + lax.broadcasted_iota(jnp.int32, (8, 64), 0)

    @pl.loop(1, 8)
    def _(k):
        came_q(k).wait_recv()

    chosen = jnp.dot(sel, queries[...].reshape(256, 256), preferred_element_type=F32)
    length = chosen[16:24, 0:1] * 128.0 + chosen[24:32, 0:1]
    length = jnp.concatenate([length, length], axis=0)
    token_span = lax.broadcasted_iota(jnp.int32, (16, 512), 1) // C
    row_span = lax.rem(lax.broadcasted_iota(jnp.int32, (16, 512), 0), CD)
    live = (token_span == row_span) & (position < length)
    span_scale = lax.rsqrt(jnp.sum(span_ss[...], axis=1, keepdims=True) / D + EPS)
    lanes = lax.broadcasted_iota(jnp.int32, (16, 128), 1)
    for j in range(2):
        at = slice(j * 128, (j + 1) * 128)
        keys = rotate(kv_acc[:, at] * span_scale, cosk[...], sink[...]).astype(BF)
        values = (kv_acc[:, 256 + j * 128:384 + j * 128] * span_scale).astype(BF)
        scores = lax.dot_general(
            chosen[0:16, at].astype(BF), keys, (((1,), (1,)), ((), ())), preferred_element_type=F32
        ) * SCALE
        scores = jnp.where(live, scores, MASKED)
        top = jnp.max(scores, axis=1, keepdims=True)
        weights = jnp.where(live, jnp.exp(scores - top), 0.0)
        total = jnp.sum(weights, axis=1, keepdims=True)
        partials[s, j * 16:(j + 1) * 16, 0:128] = jnp.dot(weights.astype(BF), values, preferred_element_type=F32)
        partials[s, j * 16:(j + 1) * 16, 128:256] = jnp.where(lanes < 64, top, total)

    def copy_p(k):
        t = at_seq(k)
        return remote(partials.at[s], partials.at[s], sp.at[t], rp.at[s], (t, h))

    def came_p(k):
        f = at_seq(8 - k)
        return remote(partials.at[f], partials.at[f], sp.at[f], rp.at[f], (f, h))

    @pl.loop(1, 8)
    def _(k):
        copy_p(k).start()

    def project_fresh(j, acc):
        return acc + jnp.dot(toks[j], wkv[j], preferred_element_type=F32)

    new_kv = lax.fori_loop(0, 16, project_fresh, jnp.zeros((16, 512), F32)) * token_scale
    for j in range(2):
        at = slice(j * 128, (j + 1) * 128)
        fresh[j] = rotate(new_kv[:, at], cosq[...], sinq[...]).astype(BF).astype(F32)
        fresh[2 + j] = new_kv[:, 256 + j * 128:384 + j * 128].astype(BF).astype(F32)

    @pl.loop(1, 8)
    def _(k):
        came_p(k).wait_recv()

    own_q = queries[s, 0:16].astype(F32)
    heads = []
    for j in range(2):
        steps = []
        for t in range(2):
            block = partials[:, pl.ds(j * 16 + t * 8, 8), :].reshape(64, 256)
            stats = block[:, 128:256].T
            tops, sums = stats[0:8], stats[64:72]
            q = own_q[t * 8:(t + 1) * 8, j * 128:(j + 1) * 128]
            fresh_scores = [
                jnp.sum(q * fresh[j, u * 8:(u + 1) * 8], axis=1, keepdims=True) * SCALE for u in range(t + 1)
            ]
            best = jnp.max(jnp.where(match, tops, MASKED), axis=1, keepdims=True)
            for score in fresh_scores:
                best = jnp.maximum(best, score)
            factor = jnp.where(match, jnp.exp(jnp.where(match, tops, best) - best), 0.0)
            total = jnp.sum(factor * sums, axis=1, keepdims=True)
            value = jnp.dot(factor, block[:, 0:128], precision=lax.Precision.HIGHEST, preferred_element_type=F32)
            for u, score in enumerate(fresh_scores):
                e = jnp.exp(score - best)
                total = total + e
                value = value + e * fresh[2 + j, u * 8:(u + 1) * 8]
            steps.append(value / total)
        heads.append(jnp.concatenate(steps, axis=0))
    att = jnp.concatenate(heads, axis=1).astype(BF)

    @pl.loop(0, 16)
    def _(j):
        weight_copy(2, j).wait()

    def copy_a(k):
        t = at_head(k)
        return remote(send_a.at[t], recv_a.at[h], sa.at[t], ra.at[h], (s, t))

    def came_a(k):
        f = at_head(16 - k)
        return remote(send_a.at[f], recv_a.at[f], sa.at[f], ra.at[f], (s, f))

    @pl.loop(1, 16)
    def _(k):
        t = at_head(k)
        send_a[t] = jnp.dot(att, wo[t], preferred_element_type=F32).astype(BF)
        copy_a(k).start()

    res[...] = tok_ref[...].astype(F32) + jnp.dot(att, wo[h], preferred_element_type=F32)

    @pl.loop(1, 16)
    def _(k):
        came_a(k).wait_recv()
        res[...] += recv_a[at_head(16 - k)].astype(F32)

    rows[h, slot] = (res[...] * own_gain[1:2]).astype(BF)

    def copy_1(k):
        t = lax.rem(s + k, 8)
        return remote(rows.at[h, slot], rows.at[h, slot], s1.at[t], r1.at[s], (t, h))

    def came_1(k):
        f = lax.rem(s + 8 - k, 8)
        place = lax.rem(f, 2) * 4 + f // 2
        return remote(rows.at[h, place], rows.at[h, place], s1.at[f], r1.at[f], (f, h))

    @pl.loop(1, 8)
    def _(k):
        copy_1(k).start()

    @pl.loop(1, 8)
    def _(k):
        came_1(k).wait_recv()

    def rows_of(block, core, half):
        return rows.at[block, pl.ds(core * 4 + half * 2, 2)]

    row_sends = []

    def spread(half, block, axis, way):
        there = place(half, way, 0) if axis == 0 else place(half, 0, way)
        where = rows_of(block, c, half)
        copy = remote(where, where, s2.at[len(row_sends)], r2.at[block, half], (s, there))
        copy.start()
        row_sends.append(copy)

    def to_pair(half, block):
        where = rows_of(block, c, half)
        return remote(where, where, s3.at[block, half], r3.at[block, half], (pair, h))

    def came(half, block):
        where = rows_of(block, c, half)
        remote(where, where, s2.at[0], r2.at[block, half], (s, h)).wait_recv()
        to_pair(half, block).start()

    for axis in range(2):
        for way in range(1, 4):
            for half in range(2):
                spread(half, h, axis, way)

    @pl.loop(0, 16)
    def _(j):
        weight_copy(3, j).wait()

    gu_acc[...] = jnp.zeros_like(gu_acc)
    row_ss[...] = jnp.zeros_like(row_ss)

    def use_rows(block):
        part = rows[block].reshape(128, 512)
        row_ss[...] += fold_squares(part.astype(F32), inv_gain[block, 1:2])
        gu_acc[...] += jnp.dot(part, wgu[block], preferred_element_type=F32)

    use_rows(h)
    for a in range(1, 4):
        for half in range(2):
            block = place(half, a, 0)
            came(half, block)
            for way in range(1, 4):
                spread(half, block, 1, way)
    done = {(0, 0)}
    for a in range(4):
        for b in range(1, 4):
            for half in range(2):
                came(half, place(half, a, b))
        for source in [(i, j) for i in range(a + 1 if a else 4) for j in range(a + 1 if a else 4)]:
            if source in done or (a == 0 and 0 not in source):
                continue
            done.add(source)
            block = place(0, *source)
            for half in range(2):
                where = rows_of(block, 1 - c, half)
                remote(where, where, s3.at[block, half], r3.at[block, half], (pair, h)).wait_recv()
            use_rows(block)

    acc = gu_acc[...]
    squares = row_ss[...]
    scale = lax.rsqrt(jnp.sum(squares, axis=1, keepdims=True) / D + EPS)
    gate = acc[:, 0:128] * scale
    up = acc[:, 128:256] * scale
    act = (gate / (1.0 + jnp.exp(-gate)) * up).astype(BF)

    def copy_d1(t):
        return remote(send_d1.at[t], recv_d1.at[t], sd1.at[t], rd1.at[t], (pair, h))

    here = (px, pz)

    def copy_e(half, k):
        mine = here[half]
        t = lax.rem(mine + k, 4)
        f = lax.rem(mine + 4 - k, 4)
        return (
            remote(send_e.at[half, t], recv_e.at[half, mine], se.at[half, t], re.at[half, mine], (s, place(half, k, 0))),
            remote(send_e.at[half, f], recv_e.at[half, f], se.at[half, f], re.at[half, f], (s, h)),
            f,
        )

    def copy_f(half, k):
        mine = here[1 - half]
        t = lax.rem(mine + k, 4)
        f = lax.rem(mine + 4 - k, 4)
        return (
            remote(send_f.at[half, t], recv_f.at[half, mine], sf.at[half, t], rf.at[half, mine], (s, place(half, 0, k))),
            remote(send_f.at[half, f], recv_f.at[half, f], sf.at[half, f], rf.at[half, f], (s, h)),
            f,
        )

    line = [(a, b) for a in (1, 2, 3, 0) for b in (1, 2, 3, 0)]
    for a, b in line:
        t = place(0, a, b)
        terms = jnp.dot(act, wd[t], preferred_element_type=F32)
        first, last = terms[0:64], terms[64:128]
        own_terms[t] = jnp.where(c == 0, first, last)
        send_d1[t] = jnp.where(c == 0, last, first).astype(BF)
        copy_d1(t).start()

    for a, b in line:
        t = place(0, a, b)
        tx, tz = lax.rem(px + a, 4), lax.rem(pz + b, 4)
        copy_d1(t).wait_recv()
        total = own_terms[t] + recv_d1[t].astype(F32)
        if a:
            send_e[0, tx, tz] = total[0:32].astype(BF)
        else:
            own_terms[t, 0:32] = total[0:32]
        if b:
            send_e[1, tz, tx] = total[32:64].astype(BF)
        else:
            own_terms[t, 32:64] = total[32:64]
        if a and b == 0:
            copy_e(0, a)[0].start()
        if a == 0 and b:
            copy_e(1, b)[0].start()

    for k in range(1, 4):
        for half in range(2):
            _, came_e, f = copy_e(half, k)
            came_e.wait_recv()
            for i in range(4):
                t = place(half, 0, i)
                at = slice(half * 32, half * 32 + 32)
                own_terms[t, at] += recv_e[half, f, lax.rem(here[1 - half] + i, 4)].astype(F32)

    for k in range(1, 4):
        for half in range(2):
            t = place(half, 0, k)
            send_f[half, lax.rem(here[1 - half] + k, 4)] = own_terms[t, half * 32:half * 32 + 32].astype(BF)
            copy_f(half, k)[0].start()

    for k in range(1, 4):
        for half in range(2):
            _, came_f, f = copy_f(half, k)
            came_f.wait_recv()
            own_terms[h, half * 32:half * 32 + 32] += recv_f[half, f].astype(F32)

    def copy_d3(k):
        t = lax.rem(y + k, 4)
        return remote(send_d3.at[t], recv_d3.at[y], sd3.at[t], rd3.at[y], (t * 2 + c, h))

    def came_d3(k):
        f = lax.rem(y + 4 - k, 4)
        return remote(send_d3.at[f], recv_d3.at[f], sd3.at[f], rd3.at[f], (f * 2 + c, h))

    send_d3[...] = own_terms[h].reshape(4, 16, 512).astype(BF)
    for k in range(1, 4):
        copy_d3(k).start()
    total = res[...] + own_terms[h, pl.ds(pl.multiple_of(y * 16, 16), 16)]
    for k in range(1, 4):
        came_d3(k).wait_recv()
        total = total + recv_d3[lax.rem(y + 4 - k, 4)].astype(F32)
    out_ref[...] = total.astype(BF)

    for copy in sends + row_sends:
        copy.wait_send()

    for k in range(1, 4):
        for half in range(2):
            copy_e(half, k)[0].wait_send()
            copy_f(half, k)[0].wait_send()

    @pl.loop(1, 16)
    def _(k):
        copy_t(k).wait_send()
        copy_a(k).wait_send()
        for half in range(2):
            to_pair(half, at_head(k)).wait_send()
        copy_d1(at_head(k)).wait_send()

    copy_d1(h).wait_send()

    @pl.loop(1, 8)
    def _(k):
        copy_1(k).wait_send()
        copy_q(k).wait_send()
        copy_p(k).wait_send()

    for k in range(1, 4):
        copy_d3(k).wait_send()


def local(
    hidden_states, span_group, span_slot, span_block, prompt_len, new_tokens, norm_gain, w_q, w_kv, w_o, w_gate_up, w_down
):
    freqs = np.tile(THETA ** (-np.arange(HD // 2) * 2.0 / HD), 2)[None, :]
    steps = np.arange(C)[:, None] * freqs
    packed_kv = w_kv.reshape(D, 2, 2, HD).transpose(0, 2, 1, 3).reshape(D * 4, HD)

    vmem = pl.BlockSpec(memory_space=pltpu.VMEM)
    smem = pl.BlockSpec(memory_space=pltpu.SMEM)
    hbm = pl.BlockSpec(memory_space=pl.ANY)
    dma = pltpu.SemaphoreType.DMA
    out = pl.pallas_call(
        layer_kernel,
        name="layer",
        out_shape=jax.ShapeDtypeStruct((16, 512), BF),
        in_specs=[vmem] * 3 + [smem] * 4 + [vmem] * 2 + [hbm] * 5,
        out_specs=vmem,
        scratch_shapes=[
            pltpu.VMEM((16, 512, 256), BF),
            pltpu.VMEM((16, 2048, 128), BF),
            pltpu.VMEM((16, 1024, 128), BF),
            pltpu.VMEM((16, 512, 512), BF),
            pltpu.VMEM((16, 256, 512), BF),
            pltpu.VMEM((16, 512, 256), BF),
            pltpu.VMEM((16, 128, 512), BF),
            pltpu.VMEM((256, 256), BF),
            pltpu.VMEM((256, 256), BF),
            pltpu.VMEM((16, 2, 512), F32),
            pltpu.VMEM((512, 128), F32),
            pltpu.VMEM((512, 128), F32),
            pltpu.VMEM((16, 128), F32),
            pltpu.VMEM((16, 128), F32),
            pltpu.VMEM((16, 512, 512), BF),
            pltpu.VMEM((512, 512), F32),
            pltpu.VMEM((512, 128), F32),
            pltpu.VMEM((16, 16, 512), BF),
            pltpu.VMEM((8, 32, 256), BF),
            pltpu.VMEM((8, 32, 256), F32),
            pltpu.VMEM((4, 16, 128), F32),
            pltpu.VMEM((16, 16, 512), BF),
            pltpu.VMEM((16, 16, 512), BF),
            pltpu.VMEM((16, 8, 16, 512), BF),
            pltpu.VMEM((16, 64, 512), F32),
            pltpu.VMEM((16, 64, 512), BF),
            pltpu.VMEM((16, 64, 512), BF),
            pltpu.VMEM((2, 4, 4, 32, 512), BF),
            pltpu.VMEM((2, 4, 4, 32, 512), BF),
            pltpu.VMEM((2, 4, 32, 512), BF),
            pltpu.VMEM((2, 4, 32, 512), BF),
            pltpu.VMEM((4, 16, 512), BF),
            pltpu.VMEM((4, 16, 512), BF),
            pltpu.VMEM((16, 512), F32),
            pltpu.VMEM((128, 256), F32),
            pltpu.VMEM((128, 128), F32),
            dma((4, 16)), dma((16,)), dma((48,)), dma((16, 4)), dma((16,)), dma((16,)), dma((8,)), dma((8,)), dma((8,)), dma((8,)),
            dma((16,)), dma((16,)), dma((8,)), dma((8,)), dma((32,)), dma((16, 2)), dma((16, 2)), dma((16, 2)),
            dma((16,)), dma((16,)), dma((2, 4)), dma((2, 4)), dma((2, 4)), dma((2, 4)), dma((4,)), dma((4,)),
        ],
        compiler_params=pltpu.CompilerParams(
            collective_id=1, has_side_effects=True, vmem_limit_bytes=60 * 2**20
        ),
    )(
        hidden_states.reshape(CD * C, 512),
        new_tokens.reshape(16, 512),
        norm_gain,
        span_group.reshape(64),
        span_slot,
        span_block,
        prompt_len,
        jnp.asarray(freqs, F32),
        jnp.asarray(np.stack([np.cos(steps), np.sin(steps)]), F32),
        w_q,
        packed_kv,
        w_o,
        w_gate_up.reshape(D * 2, HD),
        w_down,
    )
    return out.reshape(2, 8, 512)


def solution(mesh):
    placed = (
        P("seq", None, "head"),
        P(),
        P(),
        P(),
        P("seq"),
        P(None, "seq", "head"),
        P(),
        P(None, "head"),
        P(None, None, "head"),
        P("head", None),
        P(None, None, ("seq", "head")),
        P(("seq", "head"), None),
    )
    return jax.shard_map(
        local, mesh=mesh, in_specs=placed, out_specs=P(None, "seq", "head"), check_vma=False
    )
```

time: 163 us -> 120 us (0.74)
  Pallas kernels: 148 us -> 118 us
  other arithmetic: 7.94 us -> 0 us
  local copies, waits for them, and re-layouts: 6.15 us -> 1.32 us
    pallas_call x1, Pallas kernels: 148 us -> 118 us  [local(): pl.pallas_call(layer_kernel, name='layer', out_shape=jax.ShapeDtypeStruct...]
    convert_element_type x6 -> x0, other arithmetic: 3.61 us -> none  [the longest x1 0.78 us: local(): gains = norm_gain.astype(F32)]
    concatenate x4 -> x0, other arithmetic: 2.44 us -> none  [the longest x1 0.84 us: local(): jnp.concatenate([cos_k, cos_k], axis=1)]
    broadcast_in_dim x8 -> x0, local copies, waits for them, and re-layouts: 2.43 us -> none  [the longest x4 0.93 us: local(): rep_kv = jnp.broadcast_to(gains[0][:, None], (D, 4)).reshape(128, 1, 256)]
where the time goes in v3:
time: 120 us
  Pallas kernels  118 us (98%)
  local copies, waits for them, and re-layouts  1.32 us (1%)
    pallas_call x1, Pallas kernels, local(): pl.pallas_call(layer_kernel, name='layer', out_shape=jax.ShapeDtypeStruct...  118 us

profile of v3, /device:TPU:0, one launch (start us, length us, event | category | flops | bytes accessed | tf_op | source)
XLA Modules:
  0.0 119.6 jit_solution(13098466956879398086)
XLA Ops:
  0.0 118.2 %layer.1 = bf16[16,512]{1,0:T(8,128)(2,1)} custom-call(bf16[512,512]{1,0:T(8,128)(2,1)} %bitcast.12, bf16[16,512]{1,0:T(8,128)(2,1)} %bitcast.14, bf16[2,8192]{1,0:T(2,128)(2,1)} %gain_ref.1, s32[64]{0:T(128)} %bitcast.15, s32[64]{0:T(128)} %slot_ref.1, s32[64]{0:T(128)} %block_ref.1, s32[8]{0:T(128)} %length_ref.1, f32[1,128]{1,0:T(1,128)} %constant.4.clone.freq_ref, ...), custom_call_target="tpu_custom_call" | custom-call | tf_op jit(solution)/shard_map/layer/pallas_call | solution.py:624
  118.3 1.3 %copy.17 = bf16[2,8,512]{2,1,0:T(8,128)(2,1)} copy(bf16[2,8,512]{2,1,0:T(8,128)(2,1)} %bitcast.13) | data formatting | bytes 32768

commit v4 on v3

--- a/solution.py
+++ b/solution.py
@@ -31,18 +31,18 @@
 
 
 ORDER = (
-    (-1, 0), (1, 0), (0, -1), (0, 1), (2, 0), (-1, -1), (1, 1), (-1, 1), (1, -1), (0, 2),
-    (2, -1), (2, 1), (-1, 2), (1, 2), (2, 2),
+    (-1, 0), (0, -1), (0, 1), (1, 0), (0, 2), (-1, -1), (-1, 1), (2, 0), (1, -1), (1, 1),
+    (-1, 2), (2, -1), (2, 1), (1, 2), (2, 2),
 )
 
 
 def layer_kernel(
     x_ref, tok_ref, gain_ref, group_ref, slot_ref, block_ref, length_ref, freq_ref, step_ref, wq_hbm, wkv_hbm, wo_hbm, wgu_hbm, wd_hbm, out_ref,
     wq, raw, raw_gu, wkv, wo, wgu, wd, pick_kv, pick_gu, inv_gain, cosk, sink, cosq, sinq, spans, kv_acc, span_ss, toks, queries, partials, fresh,
-    send_a, recv_a, rows, own_terms, send_d1, recv_d1, send_e, recv_e, send_f, recv_f, send_d3, recv_d3, res,
+    send_a, recv_a, rows, own_terms, send_d1, recv_d1, send_e, recv_e, send_g, recv_g, res,
     gu_acc, row_ss,
     wsem, gsem, sx, rx, st, rt, sq, rq, sp, rp,
-    sa, ra, s1, r1, s2, r2, s3, r3, sd1, rd1, se, re, sf, rf, sd3, rd3,
+    sa, ra, s1, r1, s2, r2, s3, r3, sd1, rd1, se, re, sg, rg,
 ):
     s = lax.axis_index("seq")
     h = lax.axis_index("head")
@@ -59,6 +59,10 @@
     def at_seq(k):
         return lax.rem(s + k, 8)
 
+    def place(half, a, b):
+        dx, dz = (a, b) if half == 0 else (b, a)
+        return lax.rem(px + dx + 4, 4) * 4 + lax.rem(pz + dz + 4, 4)
+
     barrier = pltpu.get_barrier_semaphore()
 
     @pl.loop(1, 16)
@@ -69,40 +73,31 @@
     def _(k):
         pl.semaphore_signal(barrier, inc=1, device_id=(at_seq(k), h), device_id_type=MESH)
 
-    def weight_copy(which, j):
-        cols = pl.ds(pl.multiple_of(j * 512, 512), 512)
-        if which == 0:
-            return pltpu.make_async_copy(wkv_hbm.at[pl.ds(pl.multiple_of(j * 2048, 2048), 2048)], raw.at[j], wsem.at[0, j])
-        if which == 1:
-            return pltpu.make_async_copy(wq_hbm.at[cols], wq.at[j], wsem.at[1, j])
-        if which == 2:
-            return pltpu.make_async_copy(wo_hbm.at[:, cols], wo.at[j], wsem.at[2, j])
-        return pltpu.make_async_copy(wd_hbm.at[:, cols], wd.at[j], wsem.at[3, j])
-
-    def gate_up_copy(j):
-        return pltpu.make_async_copy(
-            wgu_hbm.at[pl.ds(pl.multiple_of(j * 1024, 1024), 1024)], raw_gu.at[j], gsem.at[j]
-        )
-
-    for which in range(4):
-        @pl.loop(0, 16)
-        def _(j):
-            weight_copy(which, j).start()
-
-    @pl.loop(0, 16)
-    def _(j):
-        gate_up_copy(j).start()
+    def at_y(k):
+        return lax.rem(y + k, 4) * 2 + c
+
+    for half in range(2):
+        @pl.loop(1, 4)
+        def _(i):
+            @pl.loop(1, 4)
+            def _(k):
+                pl.semaphore_signal(barrier, inc=1, device_id=(at_y(i), place(half, k, 0)), device_id_type=MESH)
+
+    def kv_copy(j):
+        return pltpu.make_async_copy(wkv_hbm.at[pl.ds(pl.multiple_of(j * 2048, 2048), 2048)], raw.at[j], gsem.at[j])
+
+    wq_copy = pltpu.make_async_copy(wq_hbm, wq, wsem.at[0])
+    gu_copy = pltpu.make_async_copy(wgu_hbm, raw_gu, wsem.at[1])
+    wo_copy = pltpu.make_async_copy(wo_hbm, wo, wsem.at[2])
+    wd_copy = pltpu.make_async_copy(wd_hbm, wd, wsem.at[3])
+
+    def block_at(j):
+        return pl.ds(pl.multiple_of(j * 512, 512), 512)
 
     def remote(src, dst, ssem, rsem, device):
         return pltpu.make_async_remote_copy(
             src_ref=src, dst_ref=dst, send_sem=ssem, recv_sem=rsem, device_id=device, device_id_type=MESH
         )
-
-    row = lax.broadcasted_iota(jnp.int32, (256, 256), 0)
-    col = lax.broadcasted_iota(jnp.int32, (256, 256), 1)
-    low = lax.rem(col, 4)
-    pick_kv[...] = jnp.where(row == (lax.rem(low, 2) * 2 + low // 2) * 64 + col // 4, 1.0, 0.0).astype(BF)
-    pick_gu[...] = jnp.where(row == lax.rem(col, 2) * 128 + col // 2, 1.0, 0.0).astype(BF)
 
     own_gain = gain_ref[:, pl.ds(pl.multiple_of(h * 512, 512), 512)].astype(F32)
     spans[h] = (x_ref[...].astype(F32) * own_gain[0:1]).astype(BF)
@@ -117,10 +112,7 @@
 
     lengths = per_row((8, 256), [length_ref[i] for i in range(8)])
     queries[s, 16:32] = jnp.concatenate([lengths // 128, lax.rem(lengths, 128)], axis=0).astype(F32).astype(BF)
-    kv_acc[...] = jnp.zeros_like(kv_acc)
-    span_ss[...] = jnp.zeros_like(span_ss)
-
-    pl.semaphore_wait(barrier, 22)
+    pl.semaphore_wait(barrier, 40)
 
     def make_tables():
         @pl.loop(0, 16)
@@ -151,14 +143,6 @@
         f = at_head(16 - k)
         return remote(toks.at[f], toks.at[f], st.at[f], rt.at[f], (s, f))
 
-    @pl.loop(1, 16)
-    def _(k):
-        copy_t(k).start()
-
-    def place(half, a, b):
-        dx, dz = (a, b) if half == 0 else (b, a)
-        return lax.rem(px + dx + 4, 4) * 4 + lax.rem(pz + dz + 4, 4)
-
     sends = []
 
     def push(half, block, part, axis, way):
@@ -175,7 +159,7 @@
         remote(where, where, sx.at[0], rx.at[block, half * 2 + sem], (s, h)).wait_recv()
 
     def unpack(block):
-        weight_copy(0, block).wait()
+        kv_copy(block).wait()
 
         @pl.loop(0, 4)
         def _(b):
@@ -188,11 +172,9 @@
                     wkv[block, at, pl.ds(i * 128, 128)] = got[i * 64:(i + 1) * 64, e * 128:(e + 1) * 128]
 
     def unpack_gate_up(block):
-        gate_up_copy(block).wait()
-
         @pl.loop(0, 2)
         def _(b):
-            part = raw_gu[block, pl.ds(pl.multiple_of(b * 512, 512), 512)]
+            part = raw_gu[pl.ds(pl.multiple_of(block * 1024 + b * 512, 512), 512)]
             part = jnp.concatenate([part[0:256], part[256:512]], axis=1)
             got = jnp.dot(pick_gu[...], part, preferred_element_type=F32).astype(BF)
             for i in range(2):
@@ -215,15 +197,31 @@
         for way in (1, -1):
             push(half, h, 2, 1, way)
 
+    @pl.loop(1, 16)
+    def _(k):
+        copy_t(k).start()
+
+    @pl.loop(0, 16)
+    def _(j):
+        kv_copy(at_head(j)).start()
+
+    for copy in (wq_copy, gu_copy, wo_copy, wd_copy):
+        copy.start()
+
+    row = lax.broadcasted_iota(jnp.int32, (256, 256), 0)
+    col = lax.broadcasted_iota(jnp.int32, (256, 256), 1)
+    low = lax.rem(col, 4)
+    pick_kv[...] = jnp.where(row == (lax.rem(low, 2) * 2 + low // 2) * 64 + col // 4, 1.0, 0.0).astype(BF)
+    pick_gu[...] = jnp.where(row == lax.rem(col, 2) * 128 + col // 2, 1.0, 0.0).astype(BF)
+
+    kv_acc[...] = jnp.zeros_like(kv_acc)
+    span_ss[...] = jnp.zeros_like(span_ss)
     make_tables()
     unpack(h)
     take(h)
-    unpack_gate_up(15)
 
     def project_queries():
-        @pl.loop(0, 16)
-        def _(j):
-            weight_copy(1, j).wait()
+        wq_copy.wait()
 
         @pl.loop(1, 16)
         def _(k):
@@ -233,7 +231,7 @@
             acc, ss = carry
             part = toks[j]
             ss = ss + fold_squares(part.astype(F32), inv_gain[j, 0:1])
-            return acc + jnp.dot(part, wq[j], preferred_element_type=F32), ss
+            return acc + jnp.dot(part, wq[block_at(j)], preferred_element_type=F32), ss
 
         acc, ss = lax.fori_loop(0, 16, body, (jnp.zeros((16, 256), F32), jnp.zeros((16, 128), F32)))
         scale = lax.rsqrt(jnp.sum(ss, axis=1, keepdims=True) / D + EPS)
@@ -256,10 +254,32 @@
         return remote(queries.at[f], queries.at[f], sq.at[f], rq.at[f], (f, h))
 
     arrived = [set(), set()]
+    unpacked = {(0, 0)}
     taken = {(0, 0)}
+    upcoming = []
+    for a, b in ORDER:
+        for source in ((a % 4, b % 4), (b % 4, a % 4)):
+            if source not in upcoming:
+                upcoming.append(source)
+
+    def unpack_once(source):
+        if source not in unpacked:
+            unpacked.add(source)
+            unpack(place(0, *source))
+
+    def take_ready(most):
+        for source in [u for u in upcoming if u in arrived[0] and u in arrived[1] and u not in taken][:most]:
+            taken.add(source)
+            unpack_once(source)
+            take(place(0, *source))
+
     token_scale = None
     for number, (a, b) in enumerate(ORDER):
-        ready = sorted((arrived[0] & arrived[1]) - taken)
+        if b == 2:
+            take_ready(15)
+            for source in [u for u in upcoming if u not in unpacked][:3]:
+                unpack_once(source)
+        had = sum(u in arrived[0] and u in arrived[1] and u not in taken for u in upcoming)
         for half in range(2):
             block = place(half, a, b)
             parts = (0, 1) if (a == 2 and b == 0) or b == 2 else (2,)
@@ -276,17 +296,18 @@
                 push(half, block, 0, 1, 1)
             elif b == 1:
                 push(half, block, 1, 1, -1)
+        if b != 2:
+            take_ready(min(had, 2))
+        for half in range(2):
             arrived[half].add((a % 4, b % 4) if half == 0 else (b % 4, a % 4))
-        for source in ready[:2]:
-            taken.add(source)
-            unpack(place(0, *source))
-            take(place(0, *source))
-        unpack_gate_up(number)
+        if 6 <= number <= 13:
+            if number == 6:
+                gu_copy.wait()
+            unpack_gate_up(2 * number - 12)
+            unpack_gate_up(2 * number - 11)
         if number == 3:
             token_scale = project_queries()
-    for source in sorted((arrived[0] & arrived[1]) - taken):
-        unpack(place(0, *source))
-        take(place(0, *source))
+    take_ready(15)
 
     lane = lax.broadcasted_iota(jnp.int32, (32, 256), 1)
     line = lax.broadcasted_iota(jnp.int32, (32, 256), 0)
@@ -327,8 +348,16 @@
         top = jnp.max(scores, axis=1, keepdims=True)
         weights = jnp.where(live, jnp.exp(scores - top), 0.0)
         total = jnp.sum(weights, axis=1, keepdims=True)
-        partials[s, j * 16:(j + 1) * 16, 0:128] = jnp.dot(weights.astype(BF), values, preferred_element_type=F32)
-        partials[s, j * 16:(j + 1) * 16, 128:256] = jnp.where(lanes < 64, top, total)
+        summed = jnp.dot(weights.astype(BF), values, preferred_element_type=F32)
+        partials[s, j * 16:(j + 1) * 16, 0:128] = summed.astype(BF)
+        top_high = top.astype(BF).astype(F32)
+        top_mid = (top - top_high).astype(BF).astype(F32)
+        total_high = total.astype(BF).astype(F32)
+        stats = jnp.where(lanes < 16, top_high, top_mid)
+        stats = jnp.where(lanes < 32, stats, top - top_high - top_mid)
+        stats = jnp.where(lanes < 48, stats, total_high)
+        stats = jnp.where(lanes < 64, stats, total - total_high)
+        partials[s, j * 16:(j + 1) * 16, 128:256] = stats.astype(BF)
 
     def copy_p(k):
         t = at_seq(k)
@@ -356,13 +385,14 @@
         came_p(k).wait_recv()
 
     own_q = queries[s, 0:16].astype(F32)
+    arrived_parts = [[partials[i:i + 1, j * 16:(j + 1) * 16].astype(F32) for i in range(8)] for j in range(2)]
     heads = []
     for j in range(2):
         steps = []
         for t in range(2):
-            block = partials[:, pl.ds(j * 16 + t * 8, 8), :].reshape(64, 256)
+            block = jnp.concatenate([both[:, t * 8:(t + 1) * 8] for both in arrived_parts[j]], axis=0).reshape(64, 256)
             stats = block[:, 128:256].T
-            tops, sums = stats[0:8], stats[64:72]
+            tops, sums = stats[0:8] + stats[16:24] + stats[32:40], stats[48:56] + stats[64:72]
             q = own_q[t * 8:(t + 1) * 8, j * 128:(j + 1) * 128]
             fresh_scores = [
                 jnp.sum(q * fresh[j, u * 8:(u + 1) * 8], axis=1, keepdims=True) * SCALE for u in range(t + 1)
@@ -381,9 +411,7 @@
         heads.append(jnp.concatenate(steps, axis=0))
     att = jnp.concatenate(heads, axis=1).astype(BF)
 
-    @pl.loop(0, 16)
-    def _(j):
-        weight_copy(2, j).wait()
+    wo_copy.wait()
 
     def copy_a(k):
         t = at_head(k)
@@ -393,37 +421,37 @@
         f = at_head(16 - k)
         return remote(send_a.at[f], recv_a.at[f], sa.at[f], ra.at[f], (s, f))
 
-    @pl.loop(1, 16)
-    def _(k):
-        t = at_head(k)
-        send_a[t] = jnp.dot(att, wo[t], preferred_element_type=F32).astype(BF)
-        copy_a(k).start()
-
-    res[...] = tok_ref[...].astype(F32) + jnp.dot(att, wo[h], preferred_element_type=F32)
-
-    @pl.loop(1, 16)
-    def _(k):
+    for first in range(1, 16, 5):
+        for k in range(first, first + 5):
+            t = at_head(k)
+            send_a[t] = jnp.dot(att, wo[:, block_at(t)], preferred_element_type=F32).astype(BF)
+        for k in range(first, first + 5):
+            copy_a(k).start()
+
+    summed = tok_ref[...].astype(F32) + jnp.dot(att, wo[:, block_at(h)], preferred_element_type=F32)
+    for k in range(1, 16):
         came_a(k).wait_recv()
-        res[...] += recv_a[at_head(16 - k)].astype(F32)
+        summed = summed + recv_a[at_head(16 - k)].astype(F32)
+    res[...] = summed
 
     rows[h, slot] = (res[...] * own_gain[1:2]).astype(BF)
-
-    def copy_1(k):
-        t = lax.rem(s + k, 8)
-        return remote(rows.at[h, slot], rows.at[h, slot], s1.at[t], r1.at[s], (t, h))
-
-    def came_1(k):
-        f = lax.rem(s + 8 - k, 8)
-        place = lax.rem(f, 2) * 4 + f // 2
-        return remote(rows.at[h, place], rows.at[h, place], s1.at[f], r1.at[f], (f, h))
-
-    @pl.loop(1, 8)
-    def _(k):
-        copy_1(k).start()
-
-    @pl.loop(1, 8)
-    def _(k):
-        came_1(k).wait_recv()
+    own_half = y // 2
+    own_line = jnp.where(own_half == 0, px, pz)
+
+    def copy_1(i, k):
+        there = jnp.where(own_half == 0, place(0, k, 0), place(1, k, 0))
+        where = rows.at[h, slot]
+        return remote(where, where, s1.at[i, k], r1.at[own_half, lax.rem(y, 2), own_line], (at_y(i), there))
+
+    for i in range(4):
+        for k in range(4):
+            if i or k:
+                copy_1(i, k).start()
+
+    def came_1(half, i, k):
+        where = rows.at[place(half, k, 0), c * 4 + half * 2 + i]
+        line = lax.rem((px, pz)[half] + k, 4)
+        remote(where, where, s1.at[0, 1], r1.at[half, i, line], (s, h)).wait_recv()
 
     def rows_of(block, core, half):
         return rows.at[block, pl.ds(core * 4 + half * 2, 2)]
@@ -446,14 +474,7 @@
         remote(where, where, s2.at[0], r2.at[block, half], (s, h)).wait_recv()
         to_pair(half, block).start()
 
-    for axis in range(2):
-        for way in range(1, 4):
-            for half in range(2):
-                spread(half, h, axis, way)
-
-    @pl.loop(0, 16)
-    def _(j):
-        weight_copy(3, j).wait()
+    wd_copy.wait()
 
     gu_acc[...] = jnp.zeros_like(gu_acc)
     row_ss[...] = jnp.zeros_like(row_ss)
@@ -463,27 +484,39 @@
         row_ss[...] += fold_squares(part.astype(F32), inv_gain[block, 1:2])
         gu_acc[...] += jnp.dot(part, wgu[block], preferred_element_type=F32)
 
-    use_rows(h)
-    for a in range(1, 4):
+    for k in range(4):
         for half in range(2):
-            block = place(half, a, 0)
-            came(half, block)
+            block = place(half, k, 0)
+            for i in range(2):
+                if k:
+                    came_1(half, i, k)
+                else:
+                    @pl.when(y != half * 2 + i)
+                    def _():
+                        came_1(half, i, k)
             for way in range(1, 4):
                 spread(half, block, 1, way)
-    done = {(0, 0)}
-    for a in range(4):
-        for b in range(1, 4):
-            for half in range(2):
-                came(half, place(half, a, b))
-        for source in [(i, j) for i in range(a + 1 if a else 4) for j in range(a + 1 if a else 4)]:
-            if source in done or (a == 0 and 0 not in source):
-                continue
-            done.add(source)
+            to_pair(half, block).start()
+    have = [{(k, 0) for k in range(4)}, {(0, k) for k in range(4)}]
+    used = set()
+
+    def use_ready(ready):
+        for source in ready:
+            used.add(source)
             block = place(0, *source)
             for half in range(2):
                 where = rows_of(block, 1 - c, half)
                 remote(where, where, s3.at[block, half], r3.at[block, half], (pair, h)).wait_recv()
             use_rows(block)
+
+    for a in range(4):
+        for b in range(1, 4):
+            ready = sorted((have[0] & have[1]) - used)
+            for half in range(2):
+                came(half, place(half, a, b))
+                have[half].add((a, b) if half == 0 else (b, a))
+            use_ready(ready)
+    use_ready(sorted((have[0] & have[1]) - used))
 
     acc = gu_acc[...]
     squares = row_ss[...]
@@ -507,26 +540,34 @@
             f,
         )
 
-    def copy_f(half, k):
-        mine = here[1 - half]
-        t = lax.rem(mine + k, 4)
-        f = lax.rem(mine + 4 - k, 4)
-        return (
-            remote(send_f.at[half, t], recv_f.at[half, mine], sf.at[half, t], rf.at[half, mine], (s, place(half, 0, k))),
-            remote(send_f.at[half, f], recv_f.at[half, f], sf.at[half, f], rf.at[half, f], (s, h)),
-            f,
+    def copy_g(half, i, k):
+        return remote(
+            send_g.at[half, i, k], recv_g.at[here[1 - half], y], sg.at[half, i, k], rg.at[here[1 - half], y],
+            ((half * 2 + i) * 2 + c, place(half, 0, k)),
         )
 
-    line = [(a, b) for a in (1, 2, 3, 0) for b in (1, 2, 3, 0)]
-    for a, b in line:
+    def each_g(do):
+        for k in (1, 2, 3, 0):
+            for half in range(2):
+                for i in range(2):
+                    if k:
+                        do(copy_g(half, i, k))
+                    else:
+                        @pl.when(y != half * 2 + i)
+                        def _():
+                            do(copy_g(half, i, k))
+
+    def make_terms(a, b):
         t = place(0, a, b)
-        terms = jnp.dot(act, wd[t], preferred_element_type=F32)
+        terms = jnp.dot(act, wd[:, block_at(t)], preferred_element_type=F32)
         first, last = terms[0:64], terms[64:128]
         own_terms[t] = jnp.where(c == 0, first, last)
         send_d1[t] = jnp.where(c == 0, last, first).astype(BF)
         copy_d1(t).start()
 
-    for a, b in line:
+    passed = set()
+
+    def pass_terms(a, b):
         t = place(0, a, b)
         tx, tz = lax.rem(px + a, 4), lax.rem(pz + b, 4)
         copy_d1(t).wait_recv()
@@ -539,10 +580,21 @@
             send_e[1, tz, tx] = total[32:64].astype(BF)
         else:
             own_terms[t, 32:64] = total[32:64]
-        if a and b == 0:
+        passed.add((a, b))
+        if a and {(a, k) for k in range(4)} <= passed:
             copy_e(0, a)[0].start()
-        if a == 0 and b:
+        if b and {(k, b) for k in range(4)} <= passed:
             copy_e(1, b)[0].start()
+
+    line = [
+        (1, 1), (1, 2), (1, 3), (1, 0), (2, 1), (3, 1), (0, 1), (2, 2), (2, 3), (2, 0), (3, 2), (0, 2), (3, 3), (3, 0), (0, 3), (0, 0),
+    ]
+    lag = 3
+    for number in range(16 + lag):
+        if number < 16:
+            make_terms(*line[number])
+        if number >= lag:
+            pass_terms(*line[number - lag])
 
     for k in range(1, 4):
         for half in range(2):
@@ -553,33 +605,21 @@
                 at = slice(half * 32, half * 32 + 32)
                 own_terms[t, at] += recv_e[half, f, lax.rem(here[1 - half] + i, 4)].astype(F32)
 
-    for k in range(1, 4):
+    for k in range(4):
         for half in range(2):
-            t = place(half, 0, k)
-            send_f[half, lax.rem(here[1 - half] + k, 4)] = own_terms[t, half * 32:half * 32 + 32].astype(BF)
-            copy_f(half, k)[0].start()
-
-    for k in range(1, 4):
-        for half in range(2):
-            _, came_f, f = copy_f(half, k)
-            came_f.wait_recv()
-            own_terms[h, half * 32:half * 32 + 32] += recv_f[half, f].astype(F32)
-
-    def copy_d3(k):
-        t = lax.rem(y + k, 4)
-        return remote(send_d3.at[t], recv_d3.at[y], sd3.at[t], rd3.at[y], (t * 2 + c, h))
-
-    def came_d3(k):
-        f = lax.rem(y + 4 - k, 4)
-        return remote(send_d3.at[f], recv_d3.at[f], sd3.at[f], rd3.at[f], (f * 2 + c, h))
-
-    send_d3[...] = own_terms[h].reshape(4, 16, 512).astype(BF)
-    for k in range(1, 4):
-        copy_d3(k).start()
+            for i in range(2):
+                at = half * 32 + i * 16
+                send_g[half, i, k] = own_terms[place(half, 0, k), at:at + 16].astype(BF)
+    each_g(lambda copy: copy.start())
+
     total = res[...] + own_terms[h, pl.ds(pl.multiple_of(y * 16, 16), 16)]
-    for k in range(1, 4):
-        came_d3(k).wait_recv()
-        total = total + recv_d3[lax.rem(y + 4 - k, 4)].astype(F32)
+    last_line = jnp.where(own_half == 0, pz, px)
+    for i in range(4):
+        for k in range(4):
+            if i or k:
+                line, f = lax.rem(last_line + k, 4), lax.rem(y + i, 4)
+                remote(send_g.at[0, 0, 1], recv_g.at[line, f], sg.at[0, 0, 1], rg.at[line, f], (s, h)).wait_recv()
+                total = total + recv_g[line, f].astype(F32)
     out_ref[...] = total.astype(BF)
 
     for copy in sends + row_sends:
@@ -588,7 +628,6 @@
     for k in range(1, 4):
         for half in range(2):
             copy_e(half, k)[0].wait_send()
-            copy_f(half, k)[0].wait_send()
 
     @pl.loop(1, 16)
     def _(k):
@@ -600,14 +639,18 @@
 
     copy_d1(h).wait_send()
 
+    for half in range(2):
+        to_pair(half, h).wait_send()
+    each_g(lambda copy: copy.wait_send())
+    for i in range(4):
+        for k in range(4):
+            if i or k:
+                copy_1(i, k).wait_send()
+
     @pl.loop(1, 8)
     def _(k):
-        copy_1(k).wait_send()
         copy_q(k).wait_send()
         copy_p(k).wait_send()
-
-    for k in range(1, 4):
-        copy_d3(k).wait_send()
 
 
 def local(
@@ -628,13 +671,13 @@
         in_specs=[vmem] * 3 + [smem] * 4 + [vmem] * 2 + [hbm] * 5,
         out_specs=vmem,
         scratch_shapes=[
+            pltpu.VMEM((D, 256), BF),
+            pltpu.VMEM((16, 2048, 128), BF),
+            pltpu.VMEM((2 * D, 128), BF),
+            pltpu.VMEM((16, 512, 512), BF),
+            pltpu.VMEM((256, D), BF),
             pltpu.VMEM((16, 512, 256), BF),
-            pltpu.VMEM((16, 2048, 128), BF),
-            pltpu.VMEM((16, 1024, 128), BF),
-            pltpu.VMEM((16, 512, 512), BF),
-            pltpu.VMEM((16, 256, 512), BF),
-            pltpu.VMEM((16, 512, 256), BF),
-            pltpu.VMEM((16, 128, 512), BF),
+            pltpu.VMEM((128, D), BF),
             pltpu.VMEM((256, 256), BF),
             pltpu.VMEM((256, 256), BF),
             pltpu.VMEM((16, 2, 512), F32),
@@ -647,7 +690,7 @@
             pltpu.VMEM((512, 128), F32),
             pltpu.VMEM((16, 16, 512), BF),
             pltpu.VMEM((8, 32, 256), BF),
-            pltpu.VMEM((8, 32, 256), F32),
+            pltpu.VMEM((8, 32, 256), BF),
             pltpu.VMEM((4, 16, 128), F32),
             pltpu.VMEM((16, 16, 512), BF),
             pltpu.VMEM((16, 16, 512), BF),
@@ -657,16 +700,14 @@
             pltpu.VMEM((16, 64, 512), BF),
             pltpu.VMEM((2, 4, 4, 32, 512), BF),
             pltpu.VMEM((2, 4, 4, 32, 512), BF),
-            pltpu.VMEM((2, 4, 32, 512), BF),
-            pltpu.VMEM((2, 4, 32, 512), BF),
-            pltpu.VMEM((4, 16, 512), BF),
-            pltpu.VMEM((4, 16, 512), BF),
+            pltpu.VMEM((2, 2, 4, 16, 512), BF),
+            pltpu.VMEM((4, 4, 16, 512), BF),
             pltpu.VMEM((16, 512), F32),
             pltpu.VMEM((128, 256), F32),
             pltpu.VMEM((128, 128), F32),
-            dma((4, 16)), dma((16,)), dma((48,)), dma((16, 4)), dma((16,)), dma((16,)), dma((8,)), dma((8,)), dma((8,)), dma((8,)),
-            dma((16,)), dma((16,)), dma((8,)), dma((8,)), dma((32,)), dma((16, 2)), dma((16, 2)), dma((16, 2)),
-            dma((16,)), dma((16,)), dma((2, 4)), dma((2, 4)), dma((2, 4)), dma((2, 4)), dma((4,)), dma((4,)),
+            dma((4,)), dma((16,)), dma((48,)), dma((16, 4)), dma((16,)), dma((16,)), dma((8,)), dma((8,)), dma((8,)), dma((8,)),
+            dma((16,)), dma((16,)), dma((4, 4)), dma((2, 2, 4)), dma((32,)), dma((16, 2)), dma((16, 2)), dma((16, 2)),
+            dma((16,)), dma((16,)), dma((2, 4)), dma((2, 4)), dma((2, 2, 4)), dma((4, 4)),
         ],
         compiler_params=pltpu.CompilerParams(
             collective_id=1, has_side_effects=True, vmem_limit_bytes=60 * 2**20

time: 120 us -> 114 us (0.950)
  Pallas kernels: 118 us -> 112 us
    pallas_call x1, Pallas kernels: 118 us -> 112 us  [local(): pl.pallas_call(layer_kernel, name='layer', out_shape=jax.ShapeDtypeStruct...]
where the time goes in v4:
time: 114 us; the launch traced here: 113 us
  Pallas kernels  112 us (98%)
  local copies, waits for them, and re-layouts  1.32 us (1%)
    pallas_call x1, Pallas kernels, local(): pl.pallas_call(layer_kernel, name='layer', out_shape=jax.ShapeDtypeStruct...  112 us

profile of v4, /device:TPU:0, one launch (start us, length us, event | category | flops | bytes accessed | tf_op | source)
XLA Modules:
  0.0 113.3 jit_solution(14765703593831513260)
XLA Ops:
  0.0 112.0 %layer.1 = bf16[16,512]{1,0:T(8,128)(2,1)} custom-call(bf16[512,512]{1,0:T(8,128)(2,1)} %bitcast.12, bf16[16,512]{1,0:T(8,128)(2,1)} %bitcast.14, bf16[2,8192]{1,0:T(2,128)(2,1)} %gain_ref.1, s32[64]{0:T(128)} %bitcast.15, s32[64]{0:T(128)} %slot_ref.1, s32[64]{0:T(128)} %block_ref.1, s32[8]{0:T(128)} %length_ref.1, f32[1,128]{1,0:T(1,128)} %constant.4.clone.freq_ref, ...), custom_call_target="tpu_custom_call" | custom-call | tf_op jit(solution)/shard_map/layer/pallas_call | solution.py:667
  112.0 1.3 %copy.17 = bf16[2,8,512]{2,1,0:T(8,128)(2,1)} copy(bf16[2,8,512]{2,1,0:T(8,128)(2,1)} %bitcast.13) | data formatting | bytes 32768
